TPU v7x, 512 devices: a whole 4x8x8 slice. The times are simulated.
512 devices in a mesh: ctx: 64 (over z, x, core), tp: 8 (over y).
Axes of the slice: x: 4, y: 8, z: 8, core: 2. Of those that a mesh axis runs over, the one named last changes fastest.
Arguments:
- streams: bfloat16 [3, 24576, 8192], P(None, 'ctx', 'tp'), may hold values from -6 to 6
- filters: float32 [3, 7, 8192], P(None, None, 'tp'), may hold values from -3 to 3
- out_weight: bfloat16 [8192, 4096], P('tp', 'ctx'), may hold values from -0.09375 to 0.09375
- grad_out: bfloat16 [24576, 4096], P('ctx', 'tp'), may hold values from -6 to 6
- counts: int32 [64], P('ctx'), may hold values from 192 to 384, as said below
- starts: int32 [64], P('ctx'), may hold values from 0 to 18240, as said below
Outputs:
- grad_payload: bfloat16 [3, 24576, 8192], P(None, 'ctx', 'tp')
- grad_scales: float32 [3, 256, 8192], P(None, 'ctx', 'tp')
- filter_grad: float32 [3, 7, 8192], P(None, None, 'tp')
Inputs may be any that keep to these rules, and one draw needn't show every extreme that they name: `counts`: each device holds 192 to 384 tokens; they sum to 18432; some device holds exactly 384 and some exactly 192. starts[i] is the sum of counts of devices before i.
All inputs are finite; a program needn't handle non-finite values. Where the computation divides by a largest or mean magnitude, that divisor is 1e-20 or more.
Results may differ from a plain program's by a relative error of at most 0.015.
Values may be sent and summed in bfloat16 or wider, within the bound.
A program may use at most 64 MiB of HBM per device.

v0:
```python
import jax
import jax.numpy as jnp
from jax import lax
from jax.sharding import PartitionSpec as P

TILE = 128


def passed_along(block, axis, distance):
    devices = range(lax.axis_size(axis))
    route = [(i - distance, i) for i in devices if i - distance in devices]
    return lax.ppermute(block, axis, route)


def shards(streams, filters, out_weight, grad_out, counts, starts):
    capacity = streams.shape[1]
    channels = streams.shape[2]
    taps = filters.shape[1]
    rim = taps - 1
    slots = capacity // TILE + 1
    tokens_here = counts[0]
    first_pos = starts[0]
    rowid = lax.broadcasted_iota(jnp.int32, (1, capacity, 1), 1)
    usable = rowid < tokens_here
    tail_rows = lax.dynamic_slice_in_dim(streams, tokens_here - rim, rim, 1)
    before_rows = passed_along(tail_rows, "ctx", 1)
    extended = jnp.concatenate([before_rows, streams], axis=1)
    contract = (((1,), (1,)), ((), ()))
    all_columns = lax.all_gather(grad_out, "tp", axis=1, tiled=True)
    gathered = lax.all_gather(out_weight, "ctx", axis=1, tiled=True)
    grad_gate = lax.dot_general(all_columns, gathered, contract, preferred_element_type=jnp.float32)
    grad_gate = grad_gate.astype(jnp.bfloat16).astype(jnp.float32)
    filtered = jnp.zeros((3, capacity, channels), jnp.float32)
    for j in range(taps):
        filtered = filtered + filters[:, j][:, None, :] * extended[:, rim - j : rim - j + capacity]
    others = jnp.stack(
        [filtered[1] * filtered[2], filtered[0] * filtered[2], filtered[0] * filtered[1]], axis=0
    )
    grad_conv = jnp.where(usable, grad_gate[None] * others, 0.0).astype(jnp.bfloat16)
    head_rows = grad_conv[:, :rim]
    after_rows = passed_along(head_rows, "ctx", -1)
    padded = jnp.concatenate([grad_conv, jnp.zeros((3, rim, channels), jnp.bfloat16)], axis=1)
    padded = lax.dynamic_update_slice_in_dim(padded, after_rows, tokens_here, 1)
    grad_float = grad_conv.astype(jnp.float32)
    grad_input = jnp.zeros((3, capacity, channels), jnp.float32)
    taps_terms = []
    for j in range(taps):
        grad_input = grad_input + filters[:, j][:, None, :] * padded[:, j : j + capacity]
        taps_terms.append(jnp.sum(grad_float * extended[:, rim - j : rim - j + capacity], axis=1))
    taps_local = jnp.stack(taps_terms, axis=1)
    filter_grad = lax.psum(taps_local, "ctx")
    offset = first_pos % TILE
    magnitude = jnp.where(usable, jnp.abs(grad_input), 0.0)
    placed = jnp.zeros((3, slots * TILE, channels), jnp.float32)
    placed = lax.dynamic_update_slice_in_dim(placed, magnitude, offset, 1)
    partial_max = jnp.max(placed.reshape(3, slots, TILE, channels), axis=2)
    last_slot = (offset + tokens_here - 1) // TILE
    tail_max = lax.dynamic_index_in_dim(partial_max, last_slot, 1, keepdims=False)
    head_max = partial_max[:, 0]
    from_prev = passed_along(tail_max, "ctx", 1)
    from_next = passed_along(head_max, "ctx", -1)
    slot_ids = lax.broadcasted_iota(jnp.int32, (1, slots, 1), 1)
    shared_prev = (slot_ids == 0) & (offset != 0)
    shared_next = (slot_ids == last_slot) & ((first_pos + tokens_here) % TILE != 0)
    combined = jnp.maximum(partial_max, jnp.where(shared_prev, from_prev[:, None, :], 0.0))
    combined = jnp.maximum(combined, jnp.where(shared_next, from_next[:, None, :], 0.0))
    scales = combined + 1e-06
    grad_scales = jnp.where(slot_ids <= last_slot, scales, 0.0)
    spread = jnp.repeat(scales, TILE, axis=1)
    row_scale = lax.dynamic_slice_in_dim(spread, offset, capacity, 1)
    grad_payload = jnp.where(usable, grad_input / row_scale, 0.0).astype(jnp.bfloat16)
    return (grad_payload, grad_scales, filter_grad)


def solution(mesh):
    return jax.shard_map(
        shards,
        mesh=mesh,
        in_specs=(
            P(None, "ctx", "tp"),
            P(None, None, "tp"),
            P("tp", "ctx"),
            P("ctx", "tp"),
            P("ctx"),
            P("ctx"),
        ),
        out_specs=(P(None, "ctx", "tp"), P(None, "ctx", "tp"), P(None, None, "tp")),
        check_vma=False,
    )
```

profile of v0, /device:TPU:1, one launch (start us, length us, event | category | flops | bytes accessed | tf_op | source)
XLA Modules:
  0.0 368.7 jit_solution(4808000730756435187)
XLA Ops:
  7.2 0.0 all-gather.3.cloned.1.call-start
  7.2 0.7 all-gather.3.cloned.1.call-update
  7.9 0.0 all-gather.5.cloned.1.call-start
  7.9 0.7 all-gather.5.cloned.1.call-update
  8.6 0.0 all-reduce.3.cloned.1.call-start
  9.3 0.9 constant_dynamic-slice_fusion.1
  10.3 4.5 %collective-permute-start = (bf16[3,6,1024]{2,1,0:T(8,128)(2,1)S(1)}, bf16[3,6,1024]{2,1,0:T(8,128)(2,1)S(1)}, u32[]{:S(2)}, u32[]{:S(2)}) collective-permute-start(bf16[3,6,1024]{2,1,0:T(8,128)(2,1)S(1)} %constant_dynamic-slice_fusion.1), channel_id=1, source_target_pairs={{0,8},{8,16},{16,24},{24,32},{32,40},{40,48},{48,56},{56,64},{64,7... | collective-permute-start | bytes 110600 | tf_op jit(solution)/shard_map/ppermute | solution.py:12
  15.5 1.5 fusion.22
  17.1 2.0 collective-permute-done
  19.1 11.4 %fusion.5 = f32[3,384,1024]{2,1,0:T(8,128)S(1)} fusion(bf16[3,384,1024]{2,1,0:T(8,128)(2,1)} %param.6, bf16[3,6,1024]{2,1,0:T(8,128)(2,1)S(1)} %collective-permute-done, f32[3,1024]{1,0:T(4,128)S(1)} %get-tuple-element.30, f32[3,1024]{1,0:T(4,128)S(1)} %get-tuple-element.31, f32[3,1024]{1,0:T(4,128)S(1)} %get-tuple-element.32, ...), kind=kLoop, calls=%fused_computation.25 | loop fusion | flops 44826624 | bytes 7200768 | tf_op jit(solution)/shard_map/add | solution.py:35
  30.5 2.8 slice_multiply_fusion.2
  33.3 0.0 copy-start
  33.3 29.2 %all-gather.3.cloned.1.call-done = bf16[384,4096]{1,0:T(8,128)(2,1)} async-done(((bf16[384,512]{1,0:T(8,128)(2,1)}), bf16[384,4096]{1,0:T(8,128)(2,1)}) %all-gather.3.cloned.1.call-update) | async-done | bytes 3145744 | tf_op jit(solution)/shard_map/all_gather | solution.py:29
  62.5 93.1 %all-gather.5.cloned.1.call-done = bf16[1024,4096]{0,1:T(8,128)(2,1)} async-done(((bf16[1024,64]{0,1:T(8,128)(2,1)}), bf16[1024,4096]{0,1:T(8,128)(2,1)}) %all-gather.5.cloned.1.call-update) | async-done | bytes 8388624 | tf_op jit(solution)/shard_map/all_gather | solution.py:30
  155.6 0.0 copy-start.2
  155.6 0.0 copy-start.3
  155.6 0.0 copy-start.4
  155.6 6.9 %fusion.20 = f32[384,1024]{1,0:T(8,128)S(1)} fusion(bf16[384,4096]{1,0:T(8,128)(2,1)} %all-gather.3.cloned.1.call-done, bf16[1024,4096]{0,1:T(8,128)(2,1)} %all-gather.5.cloned.1.call-done), kind=kOutput, calls=%fused_computation.49 | convolution fusion | flops 3222011904 | bytes 13107200 | tf_op jit(solution)/shard_map/dot_general | solution.py:31
  162.5 0.0 copy-done
  162.5 0.0 copy-done.2
  162.5 0.0 copy-done.3
  162.5 0.0 copy-done.4
  162.6 6.3 %fusion.12 = (f32[3,1024]{1,0:T(4,128)S(1)}, f32[3,1024]{1,0:T(4,128)S(1)}, f32[3,1024]{1,0:T(4,128)S(1)}, f32[3,1024]{1,0:T(4,128)S(1)}, f32[3,1024]{1,0:T(4,12...) fusion(bf16[3,384,1024]{2,1,0:T(8,128)(2,1)S(1)} %copy-done, ...), kind=kLoop, calls=%fused_computation.32 | loop fusion | flops 53062656 | bytes 11133312 | tf_op jit(solution)/shard_map/reduce_sum | solution.py:49
  168.8 0.0 copy-start.1
  168.9 1.4 copy-done.1
  170.2 2.1 collective-permute-start.1
  172.5 0.0 copy-start.5
  172.5 0.6 copy-done.5
  173.1 0.0 all-reduce.3.cloned.1.call-update
  173.1 1.9 concatenate.7
  175.1 0.5 collective-permute-done.1
  175.6 0.2 dynamic_update_slice.6
  175.9 6.4 %abs_select_fusion = (f32[3,384,1024]{2,1,0:T(8,128)}, f32[3,384,1024]{2,1,0:T(8,128)}) fusion(pred[384]{0:T(512)(128)(4,1)S(1)} %iota_compare_fusion, bf16[3,390,1024]{2,1,0:T(8,128)(2,1)S(1)} %dynamic_update_slice.6, f32[3,1024]{1,0:T(4,128)S(1)} %get-tuple-element.30, f32[3,1024]{1,0:T(4,128)S(1)} %get-tuple-element.31, ...), kind=kLoop, calls=%fused_computation.37 | loop fusion | flops 25952256 | bytes 26038656 | tf_op jit(solution)/shard_map/jit(_where)/select_n | solution.py:53
  182.3 3.4 broadcast_in_dim.73
  185.7 14.2 %dynamic_update_slice.7 = f32[3,512,1024]{2,1,0:T(8,128)} dynamic-update-slice(f32[3,512,1024]{2,1,0:T(8,128)} %broadcast_in_dim.73, f32[3,384,1024]{2,1,0:T(8,128)} %get-tuple-element.16, s32[]{:T(128)} %constant.43.clone.1, s32[]{:T(128)S(6)} %select_n.55, s32[]{:T(128)} %constant.43.clone.1) | dynamic-update-slice | bytes 9437188 | tf_op jit(solution)/shard_map/dynamic_update_slice | solution.py:55
  200.0 3.5 bitcast_reduce_fusion
  203.5 2.8 collective-permute-start.2
  206.4 1.9 collective-permute-start.3
  208.3 145.6 %all-reduce.3.cloned.1.call-done = f32[3,7,1024]{2,0,1:T(4,128)} async-done(((f32[3,7,1024]{2,0,1:T(4,128)}), f32[3,7,1024]{2,0,1:T(4,128)}) %all-reduce.3.cloned.1.call-update) | async-done | bytes 86032 | tf_op jit(solution)/shard_map/psum | solution.py:51
  353.9 1.6 copy.9
  355.5 0.0 collective-permute-done.2
  355.5 0.0 collective-permute-done.3
  355.5 0.7 broadcast_select_fusion
  356.3 0.8 broadcast_in_dim.79
  357.0 5.1 %select_convert_fusion = bf16[3,384,1024]{2,1,0:T(8,128)(2,1)} fusion(f32[3,384,1024]{2,1,0:T(8,128)} %get-tuple-element.17, f32[3,512,1024]{2,1,0:T(8,128)S(1)} %bitcast.54, s32[]{:T(128)S(6)} %select_n.55, pred[384]{0:T(512)(128)(4,1)S(1)} %iota_compare_fusion), kind=kLoop, calls=%fused_computation.36 | loop fusion | flops 3538944 | bytes 11796868 | tf_op jit(solution)/shard_map/convert_element_type | solution.py:71
  (18 shorter events, 0.2 us)
Async XLA Ops:
  7.2 55.3 %all-gather.3.cloned.1.call-start = ((), (), s32[]{:S(2)}) async-start(), calls=%async_computation | async-start | bytes 3538944 | tf_op jit(solution)/shard_map/all_gather | solution.py:29
  7.9 147.7 %all-gather.5.cloned.1.call-start = ((), (), s32[]{:S(2)}) async-start(), calls=%async_computation.1 | async-start | bytes 8519680 | tf_op jit(solution)/shard_map/all_gather | solution.py:30
  8.6 345.3 %all-reduce.3.cloned.1.call-start = ((), (), s32[]{:S(2)}) async-start(), calls=%async_computation.2 | async-start | bytes 229376 | tf_op jit(solution)/shard_map/psum | solution.py:51
  10.3 8.9 %collective-permute-start = (bf16[3,6,1024]{2,1,0:T(8,128)(2,1)S(1)}, bf16[3,6,1024]{2,1,0:T(8,128)(2,1)S(1)}, u32[]{:S(2)}, u32[]{:S(2)}) collective-permute-start(bf16[3,6,1024]{2,1,0:T(8,128)(2,1)S(1)} %constant_dynamic-slice_fusion.1), channel_id=1, source_target_pairs={{0,8},{8,16},{16,24},{24,32},{32,40},{40,48},{48,56},{56,64},{64,7... | collective-permute-start | bytes 110600 | tf_op jit(solution)/shard_map/ppermute | solution.py:12
  33.3 129.2 %copy-start = (bf16[3,384,1024]{2,1,0:T(8,128)(2,1)S(1)}, bf16[3,384,1024]{2,1,0:T(8,128)(2,1)}, u32[]{:S(2)}) copy-start(bf16[3,384,1024]{2,1,0:T(8,128)(2,1)} %param.6) | copy-start | bytes 7077892
  155.6 6.9 %copy-start.2 = (f32[1,384,1024]{2,1,0:T(8,128)S(1)}, f32[1,384,1024]{2,1,0:T(8,128)}, u32[]{:S(2)}) copy-start(f32[1,384,1024]{2,1,0:T(8,128)} %get-tuple-element.18) | copy-start | bytes 4718596
  155.6 6.9 %copy-start.3 = (f32[1,384,1024]{2,1,0:T(8,128)S(1)}, f32[1,384,1024]{2,1,0:T(8,128)}, u32[]{:S(2)}) copy-start(f32[1,384,1024]{2,1,0:T(8,128)} %get-tuple-element.19) | copy-start | bytes 4718596
  155.6 6.9 %copy-start.4 = (f32[1,384,1024]{2,1,0:T(8,128)S(1)}, f32[1,384,1024]{2,1,0:T(8,128)}, u32[]{:S(2)}) copy-start(f32[1,384,1024]{2,1,0:T(8,128)} %get-tuple-element.20) | copy-start | bytes 4718596
  168.8 1.4 copy-start.1
  170.2 5.4 %collective-permute-start.1 = (bf16[3,6,1024]{2,1,0:T(8,128)(2,1)S(1)}, bf16[3,6,1024]{2,1,0:T(8,128)(2,1)S(1)}, u32[]{:S(2)}, u32[]{:S(2)}) collective-permute-start(bf16[3,6,1024]{2,1,0:T(8,128)(2,1)S(1)} %slice.129), channel_id=1, source_target_pairs={{8,0},{16,8},{24,16},{32,24},{40,32},{48,40},{56,48},{64,56},{72,6... | collective-permute-start | bytes 110600 | tf_op jit(solution)/shard_map/ppermute | solution.py:12
  172.5 0.6 copy-start.5
  203.5 152.0 %collective-permute-start.2 = (f32[3,1024]{1,0:T(4,128)S(1)}, f32[3,1024]{1,0:T(4,128)S(1)}, u32[]{:S(2)}, u32[]{:S(2)}) collective-permute-start(f32[3,1024]{1,0:T(4,128)S(1)} %bitcast.57), channel_id=1, source_target_pairs={{0,8},{8,16},{16,24},{24,32},{32,40},{40,48},{48,56},{56,64},{64,7... | collective-permute-start | bytes 36872 | tf_op jit(solution)/shard_map/ppermute | solution.py:12
  206.4 149.2 %collective-permute-start.3 = (f32[3,1024]{1,0:T(4,128)S(1)}, f32[3,1024]{1,0:T(4,128)S(1)}, u32[]{:S(2)}, u32[]{:S(2)}) collective-permute-start(f32[3,1024]{1,0:T(4,128)S(1)} %bitcast.58), channel_id=1, source_target_pairs={{8,0},{16,8},{24,16},{32,24},{40,32},{48,40},{56,48},{64,56},{72,6... | collective-permute-start | bytes 36872 | tf_op jit(solution)/shard_map/ppermute | solution.py:12
Sparse Core Ops, SparseCore 0:
  10.1 52.3 all-gather.2
  65.8 89.7 all-gather.4
  173.3 180.6 all-reduce.2
where the time goes:
time: 369 us
  waiting for transfers between devices  272 us (74%)
  other arithmetic  36.1 us (10%)
  local copies, waits for them, and re-layouts  26.8 us (7%)
  between operations  15.4 us (4%)
  starting transfers between devices  11.5 us (3%)
  matrix products  6.9 us (2%)
    psum x1, waiting for transfers between devices, shards(): filter_grad = lax.psum(taps_local, 'ctx')  146 us
    all_gather x1, waiting for transfers between devices, shards(): gathered = lax.all_gather(out_weight, 'ctx', axis=1, tiled=True)  93.1 us
    all_gather x1, waiting for transfers between devices, shards(): all_columns = lax.all_gather(grad_out, 'tp', axis=1, tiled=True)  29.2 us
    dynamic_update_slice x1, local copies, waits for them, and re-layouts, shards(): placed = lax.dynamic_update_slice_in_dim(placed, magnitude, offset, 1)  14.2 us
    ppermute x4, starting transfers between devices, passed_along(): return lax.ppermute(block, axis, route)  11.4 us
    add x1, other arithmetic, shards(): filtered + filters[:, j][:, None, :] * extended[:, rim - j:rim - j + capa...  11.4 us
  transfers between devices with their start and end apart: 7, of which 5 were waited for; matrix products, arithmetic and copies ran while one was open for 13% of the time, Pallas kernels for 0%

commit v1 on v0

v1 whole, which is shorter than its diff:
```python
import functools

import jax
import jax.numpy as jnp
from jax import lax
from jax.experimental import pallas as pl
from jax.experimental.pallas import tpu as pltpu
from jax.sharding import PartitionSpec as P

MESH = pl.DeviceIdType.MESH
TILE = 128
LANES = 128
NZ, NX, NC, NY = 8, 4, 2, 8
NG = NX * NC
CH = 64
SLOTS = 4


def kernel(
    streams_ref, filters_ref, weight_ref, grad_ref, counts_ref, starts_ref,
    pay_ref, scales_ref, fgrad_ref,
    sv, u32, prod, wt, gg, dy32, dc32, du32, tail, halo, head, heads_in, zbuf,
    msc, isc, tmx, max_prev, max_next, fsc, p1, p2, tot,
    send, recv, local,
):
    rows = grad_ref.shape[0]
    width = grad_ref.shape[1]
    taps = filters_ref.shape[1]
    groups = weight_ref.shape[0] // LANES
    i = lax.axis_index("ctx")
    y = lax.axis_index("tp")
    z = i // NG
    q = i % NG
    x = q // NC
    core = q % NC
    n_ctx = NZ * NG

    count = counts_ref[0]
    first = starts_ref[0]
    offset = first % TILE
    last_slot = jnp.clip((offset + count - 1) // TILE, 0, SLOTS - 1)

    def at(zz, xx, cc):
        return ((zz + NZ) % NZ) * NG + ((xx + NX) % NX) * NC + cc

    copies = []

    def push(src, dst, ctx, tp):
        k = len(copies)
        c = pltpu.make_async_remote_copy(
            src_ref=src, dst_ref=dst, send_sem=send.at[k], recv_sem=recv.at[k],
            device_id=(ctx, tp), device_id_type=MESH,
        )
        c.start()
        copies.append(c)
        return c

    up, down = (i + 1) % n_ctx, (i + n_ctx - 1) % n_ctx
    yr, yl = (y + 1) % NY, (y + NY - 1) % NY
    zr, zl = at(z + 1, x, core), at(z - 1, x, core)
    xr, xl = at(z, x + 1, core), at(z, x - 1, core)
    mate = at(z, x, 1 - core)

    get_streams = pltpu.make_async_copy(streams_ref, sv, local.at[0])
    get_streams.start()
    own_cols = pl.ds(pl.multiple_of(y * width, width), width)
    get_grad = pltpu.make_async_copy(grad_ref, gg.at[:, own_cols], local.at[1])
    get_grad.start()

    barrier = pltpu.get_barrier_semaphore()
    peers = [(i, yr), (i, yl), (up, y), (down, y)]
    peers += [(z * NG + (q + d) % NG, y) for d in range(1, NG)]
    peers += [(((z + d) % NZ) * NG + q, y) for d in range(1, NZ)]
    for peer in peers:
        pl.semaphore_signal(barrier, inc=1, device_id=peer, device_id_type=MESH)
    wt[z, x, core] = weight_ref[...].T
    pl.semaphore_wait(barrier, len(peers))

    half = rows // 2

    def gblock(c, t):
        t = (t + NY) % NY
        return gg.at[pl.ds(c * half, half), pl.ds(pl.multiple_of(t * width, width), width)]

    def gstep(c, d):
        out = []
        if d < 4 or c == 0:
            src = gblock(c, y - d + 1) if d > 1 else grad_ref.at[pl.ds(c * half, half)]
            out.append(push(src, gblock(c, y - d + 1), i, yr))
        if d < 4 or c == 1:
            src = gblock(c, y + d - 1) if d > 1 else grad_ref.at[pl.ds(c * half, half)]
            out.append(push(src, gblock(c, y + d - 1), i, yl))
        return out

    def arrived(cs):
        for c in cs:
            c.wait_recv()

    def ablock(zz, lo=0, n=NX):
        return wt.at[(zz + NZ) % NZ, pl.ds(lo, n), core, pl.ds(0, 32), :]

    def bpiece(zz, lo=32, n=32):
        return wt.at[(zz + NZ) % NZ, x, core, pl.ds(lo, n), :]

    def bblock(xx, lo=0, n=NZ):
        return wt.at[pl.ds(lo, n), (xx + NX) % NX, core, pl.ds(32, 32), :]

    def bstep(d):
        n = 32 if d < 4 else 16
        lo = 32 if d < 4 else 48
        return [
            push(bpiece(z - d + 1, 32, n), bpiece(z - d + 1, 32, n), zr, y),
            push(bpiece(z + d - 1, lo, n), bpiece(z + d - 1, lo, n), zl, y),
        ]

    def astep(d):
        n = NX if d < 4 else NX // 2
        lo = 0 if d < 4 else NX // 2
        return [
            push(ablock(z - d + 1, 0, n), ablock(z - d + 1, 0, n), zr, y),
            push(ablock(z + d - 1, lo, n), ablock(z + d - 1, lo, n), zl, y),
        ]

    g0 = gstep(0, 1)
    own = wt.at[z, x, core, pl.ds(0, 32), :]
    a1 = [push(own, own, at(z, x + d, core), y) for d in range(1, NX)]
    b1 = bstep(1)
    g1 = gstep(1, 1)

    get_streams.wait()

    def widen(cg, _):
        lanes = pl.ds(pl.multiple_of(cg * LANES, LANES), LANES)
        for s in range(3):
            u32[s, cg, 8 : 8 + rows, :] = sv[s, :, lanes].astype(jnp.float32)
            tail[s, cg] = u32[s, cg, pl.ds(jnp.clip(count, 8, rows), 8), :]
        return 0

    lax.fori_loop(0, groups, widen, 0)
    tails = push(tail, halo, up, y)

    arrived(b1)
    b2 = bstep(2)
    arrived(a1)
    mates = [push(ablock(z), ablock(z), mate, y)]
    a2 = astep(1)
    arrived(b2)
    b3 = bstep(3)
    arrived(g0)
    g0 = gstep(0, 2)
    arrived(b3)
    b4 = bstep(4)
    arrived(b4)
    bx = [push(bblock(x), bblock(x), xr, y), push(bblock(x), bblock(x), xl, y)]
    mates.append(push(bblock(x), bblock(x), mate, y))

    tails.wait_recv()

    def forward(cg, _):
        lanes = pl.ds(pl.multiple_of(cg * LANES, LANES), LANES)
        coef = []
        for s in range(3):
            u32[s, cg, 0:8, :] = jnp.where(i > 0, halo[s, cg], 0.0)
            du32[s, cg, 0:TILE, :] = jnp.zeros((TILE, LANES), jnp.float32)
            du32[s, cg, TILE + rows :, :] = jnp.zeros((TILE, LANES), jnp.float32)
            dc32[s, cg, rows:, :] = jnp.zeros((8, LANES), jnp.float32)
            zbuf[s, cg] = jnp.zeros((24, LANES), jnp.float32)
            coef.append([filters_ref[s, pl.ds(j, 1), lanes] for j in range(taps)])

        def chunk(r, _):
            r0 = pl.multiple_of(r * CH, CH)
            c = []
            for s in range(3):
                acc = coef[s][0] * u32[s, cg, pl.ds(8 + r0, CH), :]
                for j in range(1, taps):
                    acc = acc + coef[s][j] * u32[s, cg, pl.ds(8 + r0 - j, CH), :]
                c.append(acc)
            prod[0, cg, pl.ds(r0, CH), :] = c[1] * c[2]
            prod[1, cg, pl.ds(r0, CH), :] = c[0] * c[2]
            prod[2, cg, pl.ds(r0, CH), :] = c[0] * c[1]
            return 0

        lax.fori_loop(0, rows // CH, chunk, 0)
        return 0

    lax.fori_loop(0, groups, forward, 0)

    arrived(g1)
    g1 = gstep(1, 2)
    for d in range(1, 4):
        arrived(a2)
        if d == 3:
            arrived(bx)
            mates.append(push(bblock(x - 1), bblock(x - 1), mate, y))
            mates.append(push(bblock(x + 1), bblock(x + 1), mate, y))
            bx = [
                push(bblock(x - 1, 0, 4), bblock(x - 1, 0, 4), xr, y),
                push(bblock(x + 1, 4, 4), bblock(x + 1, 4, 4), xl, y),
            ]
        a2 = astep(d + 1)
        mates.append(push(ablock(z - d), ablock(z - d), mate, y))
        mates.append(push(ablock(z + d), ablock(z + d), mate, y))
        if d < 3:
            arrived(g0)
            g0 = gstep(0, d + 2)
            arrived(g1)
            g1 = gstep(1, d + 2)
    arrived(a2)
    mates.append(push(ablock(z + 4), ablock(z + 4), mate, y))
    arrived(bx)
    mates.append(push(bblock(x + 2), bblock(x + 2), mate, y))
    get_grad.wait()
    arrived(mates)
    arrived(g0)
    arrived(g1)

    def project(n, _):
        cols = pl.ds(pl.multiple_of(n * 256, 256), 256)
        w = wt[:, :, :, :, cols].reshape(NZ * NG * 64, 256)
        dy = jnp.dot(gg[...], w, preferred_element_type=jnp.float32)
        dy = dy.astype(jnp.bfloat16).astype(jnp.float32)
        dy32[2 * n] = dy[:, :LANES]
        dy32[2 * n + 1] = dy[:, LANES:]
        return 0

    lax.fori_loop(0, groups // 2, project, 0)

    def gate(cg, _):
        def chunk(r, _):
            r0 = pl.multiple_of(r * CH, CH)
            live = lax.broadcasted_iota(jnp.int32, (CH, LANES), 0) + r0 < count
            dy = dy32[cg, pl.ds(r0, CH), :]
            for s in range(3):
                dc = jnp.where(live, dy * prod[s, cg, pl.ds(r0, CH), :], 0.0)
                dc32[s, cg, pl.ds(r0, CH), :] = dc.astype(jnp.bfloat16).astype(jnp.float32)
            return 0

        lax.fori_loop(0, rows // CH, chunk, 0)
        for s in range(3):
            head[s, cg] = dc32[s, cg, 0:8, :]
        return 0

    lax.fori_loop(0, groups, gate, 0)
    heads = push(head, heads_in, down, y)

    def correlate(cg, _):
        for s in range(3):
            def chunk(r, acc):
                r0 = pl.multiple_of(r * CH, CH)
                dc = dc32[s, cg, pl.ds(r0, CH), :]
                out = []
                for j in range(taps):
                    term = dc * u32[s, cg, pl.ds(8 + r0 - j, CH), :]
                    out.append(acc[j] + term.reshape(CH // 8, 8, LANES).sum(0))
                return tuple(out)

            zero = jnp.zeros((8, LANES), jnp.float32)
            acc = lax.fori_loop(0, rows // CH, chunk, (zero,) * taps)
            fsc[cg, s] = zero
            for j in range(taps):
                fsc[cg, s, j : j + 1, :] = acc[j].sum(0, keepdims=True)
        return 0

    lax.fori_loop(0, groups, correlate, 0)
    f1 = []
    for d in range(1, NG):
        to = (q + d) % NG
        f1.append(push(fsc.at[to], p1.at[d], z * NG + to, y))

    heads.wait_recv()

    def backward(cg, _):
        lanes = pl.ds(pl.multiple_of(cg * LANES, LANES), LANES)
        for s in range(3):
            zbuf[s, cg, 8:16, :] = jnp.where(i < n_ctx - 1, heads_in[s, cg], 0.0)

        def insert(r, _):
            r0 = pl.multiple_of(r * 8, 8)
            at_row = jnp.clip(r0 - count, -8, 8) + 8
            for s in range(3):
                dc32[s, cg, pl.ds(r0, 8), :] += zbuf[s, cg, pl.ds(at_row, 8), :]
            return 0

        lax.fori_loop(rows // 16, rows // 8 + 1, insert, 0)
        coef = [[filters_ref[s, pl.ds(j, 1), lanes] for j in range(taps)] for s in range(3)]

        def chunk(r, _):
            r0 = pl.multiple_of(r * CH, CH)
            live = lax.broadcasted_iota(jnp.int32, (CH, LANES), 0) + r0 < count
            for s in range(3):
                acc = coef[s][0] * dc32[s, cg, pl.ds(r0, CH), :]
                for j in range(1, taps):
                    acc = acc + coef[s][j] * dc32[s, cg, pl.ds(r0 + j, CH), :]
                du32[s, cg, pl.ds(TILE + r0, CH), :] = jnp.where(live, acc, 0.0)
            return 0

        lax.fori_loop(0, rows // CH, chunk, 0)

        for s in range(3):
            for k in range(SLOTS):
                block = jnp.abs(du32[s, cg, pl.ds((k + 1) * TILE - offset, TILE), :])
                top = block.reshape(TILE // 8, 8, LANES).max(0).max(0, keepdims=True)
                msc[k, pl.ds(s * groups + cg, 1), :] = top
        return 0

    lax.fori_loop(0, groups, backward, 0)
    tmx[...] = msc[last_slot]
    to_next = push(tmx, max_prev, up, y)
    to_prev = push(msc.at[0], max_next, down, y)

    arrived(f1)
    part = fsc[q]
    for d in range(1, NG):
        part = part + p1[d]
    p2[z] = part
    f2 = []
    for d in range(1, NZ):
        f2.append(push(p2.at[z], p2.at[z], ((z + d) % NZ) * NG + q, y))

    to_next.wait_recv()
    to_prev.wait_recv()
    prev = jnp.where(offset != 0, max_prev[...], 0.0)
    follow = jnp.where((first + count) % TILE != 0, max_next[...], 0.0)
    for k in range(SLOTS):
        top = msc[k]
        if k == 0:
            top = jnp.maximum(top, prev)
        top = jnp.maximum(top, jnp.where(last_slot == k, follow, 0.0))
        scale = top + 1e-6
        isc[k] = 1.0 / scale
        scale = jnp.where(last_slot >= k, scale, 0.0)
        for s in range(3):
            for cg in range(groups):
                row = s * groups + cg
                scales_ref[s, k : k + 1, cg * LANES : (cg + 1) * LANES] = scale[row : row + 1]

    def finish(cg, _):
        lanes = pl.ds(pl.multiple_of(cg * LANES, LANES), LANES)
        inv = [[isc[k, pl.ds(s * groups + cg, 1), :] for k in range(SLOTS)] for s in range(3)]

        def chunk(r, _):
            r0 = pl.multiple_of(r * CH, CH)
            pos = lax.broadcasted_iota(jnp.int32, (CH, LANES), 0) + (r0 + offset)
            for s in range(3):
                scale = jnp.where(pos >= 3 * TILE, inv[s][3], inv[s][2])
                scale = jnp.where(pos >= 2 * TILE, scale, inv[s][1])
                scale = jnp.where(pos >= TILE, scale, inv[s][0])
                du = du32[s, cg, pl.ds(TILE + r0, CH), :]
                pay_ref[s, pl.ds(r0, CH), lanes] = (du * scale).astype(jnp.bfloat16)
            return 0

        lax.fori_loop(0, rows // CH, chunk, 0)
        return 0

    lax.fori_loop(0, groups // 2, finish, 0)

    arrived(f2)
    total = p2[0]
    for d in range(1, NZ):
        total = total + p2[d]
    tot[q] = total
    f3 = []
    for d in range(1, NG):
        f3.append(push(tot.at[q], tot.at[q], z * NG + (q + d) % NG, y))

    lax.fori_loop(groups // 2, groups, finish, 0)

    arrived(f3)
    for cg in range(groups):
        for s in range(3):
            fgrad_ref[s, :, cg * LANES : (cg + 1) * LANES] = tot[cg, s, :taps, :]
    for c in copies:
        c.wait_send()


def shards(streams, filters, out_weight, grad_out, counts, starts):
    _, rows, channels = streams.shape
    taps = filters.shape[1]
    width = grad_out.shape[1]
    g = channels // LANES
    vmem = pl.BlockSpec(memory_space=pltpu.VMEM)
    anywhere = pl.BlockSpec(memory_space=pl.ANY)
    smem = pl.BlockSpec(memory_space=pltpu.SMEM)
    f32, bf16 = jnp.float32, jnp.bfloat16
    V = pltpu.VMEM
    return pl.pallas_call(
        kernel,
        out_shape=(
            jax.ShapeDtypeStruct((3, rows, channels), bf16),
            jax.ShapeDtypeStruct((3, SLOTS, channels), f32),
            jax.ShapeDtypeStruct((3, taps, channels), f32),
        ),
        in_specs=[anywhere, vmem, vmem, anywhere, smem, smem],
        out_specs=(vmem, vmem, vmem),
        scratch_shapes=[
            V((3, rows, channels), bf16),
            V((3, g, rows + 8, LANES), f32),
            V((3, g, rows, LANES), f32),
            V((NZ, NX, NC, 64, channels), bf16),
            V((rows, NY * width), bf16),
            V((g, rows, LANES), f32),
            V((3, g, rows + 8, LANES), f32),
            V((3, g, rows + 2 * TILE, LANES), f32),
            V((3, g, 8, LANES), f32),
            V((3, g, 8, LANES), f32),
            V((3, g, 8, LANES), f32),
            V((3, g, 8, LANES), f32),
            V((3, g, 24, LANES), f32),
            V((SLOTS, 3 * g, LANES), f32),
            V((SLOTS, 3 * g, LANES), f32),
            V((3 * g, LANES), f32),
            V((3 * g, LANES), f32),
            V((3 * g, LANES), f32),
            V((g, 3, 8, LANES), f32),
            V((NG, 3, 8, LANES), f32),
            V((NZ, 3, 8, LANES), f32),
            V((g, 3, 8, LANES), f32),
            pltpu.SemaphoreType.DMA((80,)),
            pltpu.SemaphoreType.DMA((80,)),
            pltpu.SemaphoreType.DMA((2,)),
        ],
        compiler_params=pltpu.CompilerParams(
            collective_id=0, has_side_effects=True, vmem_limit_bytes=60 * 1024 * 1024
        ),
        cost_estimate=pl.CostEstimate(
            flops=2 * rows * channels * NY * width, bytes_accessed=12 * rows * channels, transcendentals=0
        ),
    )(streams, filters, out_weight, grad_out, counts, starts)


def solution(mesh):
    return jax.shard_map(
        shards,
        mesh=mesh,
        in_specs=(
            P(None, "ctx", "tp"),
            P(None, None, "tp"),
            P("tp", "ctx"),
            P("ctx", "tp"),
            P("ctx"),
            P("ctx"),
        ),
        out_specs=(P(None, "ctx", "tp"), P(None, "ctx", "tp"), P(None, None, "tp")),
        check_vma=False,
    )
```

time: 369 us -> 91.8 us (0.25)
  waiting for transfers between devices: 272 us -> 0 us
  Pallas kernels: 0 us -> 83.3 us
  other arithmetic: 36.1 us -> 0 us
  local copies, waits for them, and re-layouts: 26.8 us -> 6.32 us
  between operations: 15.4 us -> 1.95 us
  starting transfers between devices: 11.5 us -> 0 us
  matrix products: 6.9 us -> 0 us
    psum x1 -> x0, waiting for transfers between devices: 146 us -> none  [shards(): filter_grad = lax.psum(taps_local, 'ctx')]
    all_gather x2 -> x0, waiting for transfers between devices: 122 us -> none  [the longest x1 93.1 us: shards(): gathered = lax.all_gather(out_weight, 'ctx', axis=1, tiled=True)]
    pallas_call x0 -> x1, Pallas kernels: none -> 83.3 us  [shards(): pl.pallas_call(kernel, out_shape=(jax.ShapeDtypeStruct((3, rows, channels...]
    dynamic_update_slice x2 -> x0, local copies, waits for them, and re-layouts: 14.5 us -> none  [the longest x1 14.2 us: shards(): placed = lax.dynamic_update_slice_in_dim(placed, magnitude, offset, 1)]
    ppermute x4 -> x0, starting transfers between devices: 11.4 us -> none  [passed_along(): return lax.ppermute(block, axis, route)]
    add x1 -> x0, other arithmetic: 11.4 us -> none  [shards(): filtered + filters[:, j][:, None, :] * extended[:, rim - j:rim - j + capa...]
    select_n x2 -> x0, other arithmetic: 7.14 us -> none  [the longest x1 6.42 us: shards(): magnitude = jnp.where(usable, jnp.abs(grad_input), 0.0)]
    dot_general x1 -> x0, matrix products: 6.9 us -> none  [shards(): lax.dot_general(all_columns, gathered, contract, preferred_element_type=j...]
  transfers between devices with their start and end apart: 7 -> 0, of which waited for: 5 -> 0; matrix products, arithmetic and copies ran while one was open for 13% -> 0% of each run, Pallas kernels for 0% -> 0%
where the time goes in v1:
time: 91.8 us; the launch traced here: 91.6 us
  Pallas kernels  83.3 us (91%)
  local copies, waits for them, and re-layouts  6.32 us (7%)
  between operations  1.95 us (2%)
    pallas_call x1, Pallas kernels, shards(): pl.pallas_call(kernel, out_shape=(jax.ShapeDtypeStruct((3, rows, channels...  83.3 us
    unnamed x8, local copies, waits for them, and re-layouts  6.32 us

profile of v1, /device:TPU:1, one launch (start us, length us, event | category | flops | bytes accessed | tf_op | source)
XLA Modules:
  0.0 91.6 jit_solution(872727313877179090)
XLA Ops:
  1.9 1.7 %copy.9.weight_ref = bf16[1024,64]{1,0:T(8,128)(2,1)} copy(bf16[1024,64]{0,1:T(8,128)(2,1)} %param.8) | data formatting | bytes 262144 | tf_op args[2]
  3.7 83.3 %shard_map.85 = (bf16[3,384,1024]{2,1,0:T(8,128)(2,1)}, f32[3,4,1024]{2,1,0:T(4,128)}, f32[3,7,1024]{2,1,0:T(8,128)}) custom-call(bf16[3,384,1024]{2,1,0:T(8,128)(2,1)} %streams_ref.1, f32[3,7,1024]{2,1,0:T(8,128)} %filters_ref.1, bf16[1024,64]{1,0:T(8,128)(2,1)} %copy.9.weight_ref, bf16[384,512]{1,0:T(8,128)(2,1)} %grad_ref.1, s32[1]{0:T(128)S(6)} %copy.13.counts_ref, ...), custom_call_target="tpu_custom_call" | custom-call | flops 3221225472 | bytes 4718592 | tf_op jit(solution)/shard_map/pallas_call | solution.py:386
  87.0 0.0 copy-start.1
  87.0 0.0 copy-start
  87.0 3.3 %copy.15 = bf16[3,384,1024]{2,1,0:T(8,128)(2,1)} copy(bf16[3,384,1024]{2,1,0:T(8,128)(2,1)} %get-tuple-element.6) | data formatting | bytes 4718592
  90.3 0.0 copy-done.1
  90.3 0.6 copy.16
  91.0 0.0 copy-done
  91.0 0.6 copy.17
Async XLA Ops:
  87.0 3.3 %copy-start.1 = (f32[3,4,1024]{2,1,0:T(4,128)S(1)}, f32[3,4,1024]{2,1,0:T(4,128)}, u32[]{:S(2)}) copy-start(f32[3,4,1024]{2,1,0:T(4,128)} %get-tuple-element.7) | copy-start | bytes 147460
  87.0 3.9 %copy-start = (f32[3,7,1024]{2,1,0:T(8,128)S(1)}, f32[3,7,1024]{2,1,0:T(8,128)}, u32[]{:S(2)}) copy-start(f32[3,7,1024]{2,1,0:T(8,128)} %get-tuple-element.8) | copy-start | bytes 258052

commit v2 on v1

v2 whole, which is shorter than its diff:
```python
import functools

import jax
import jax.numpy as jnp
from jax import lax
from jax.experimental import pallas as pl
from jax.experimental.pallas import tpu as pltpu
from jax.sharding import PartitionSpec as P

MESH = pl.DeviceIdType.MESH
TILE = 128
LANES = 128
NZ, NX, NC, NY = 8, 4, 2, 8
NG = NX * NC
CH = 64
SLOTS = 4
VLIM = 44


ORDER = (
    "b1", "f", "b2", "a0", "g01", "f", "f", "f", "x0", "f", "b3", "f", "g11", "x1", "A01", "x2",
    "A11", "f", "b4", "g02", "f", "A02", "x3", "g12", "A12", "x4", "A03", "g03", "X", "A13", "g13",
    "A04", "A14",
)


def kernel(
    streams_ref, filters_ref, weight_ref, grad_ref, counts_ref, starts_ref,
    du32, inv_ref, scales_ref, fgrad_ref,
    sv, u32, prod, wt, gg, dc32, tail, halo, head, heads_in, zbuf,
    msc, tmx, max_prev, max_next, fsc, p1, p2,
    send, recv, local,
):
    rows = grad_ref.shape[0]
    width = grad_ref.shape[1]
    taps = filters_ref.shape[1]
    groups = weight_ref.shape[1] // LANES
    i = lax.axis_index("ctx")
    y = lax.axis_index("tp")
    z = i // NG
    q = i % NG
    x = q // NC
    core = q % NC
    n_ctx = NZ * NG

    count = counts_ref[0]
    first = starts_ref[0]
    offset = first % TILE
    last_slot = jnp.clip((offset + count - 1) // TILE, 0, SLOTS - 1)

    def at(zz, xx, cc):
        return ((zz + NZ) % NZ) * NG + ((xx + NX) % NX) * NC + cc

    copies = []

    def push(src, dst, ctx, tp):
        k = len(copies)
        c = pltpu.make_async_remote_copy(
            src_ref=src, dst_ref=dst, send_sem=send.at[k], recv_sem=recv.at[k],
            device_id=(ctx, tp), device_id_type=MESH,
        )
        c.start()
        copies.append(c)
        return c

    up, down = (i + 1) % n_ctx, (i + n_ctx - 1) % n_ctx
    yr, yl = (y + 1) % NY, (y + NY - 1) % NY
    zr, zl = at(z + 1, x, core), at(z - 1, x, core)
    xr, xl = at(z, x + 1, core), at(z, x - 1, core)
    mate = at(z, x, 1 - core)

    get_streams = pltpu.make_async_copy(streams_ref, sv, local.at[0])
    get_streams.start()
    own_cols = pl.ds(pl.multiple_of(y * width, width), width)
    get_grad = pltpu.make_async_copy(grad_ref, gg.at[:, own_cols], local.at[1])
    get_grad.start()

    barrier = pltpu.get_barrier_semaphore()
    peers = [(i, yr), (i, yl), (up, y), (down, y)]
    peers += [(z * NG + (q + d) % NG, y) for d in range(1, NG)]
    peers += [(((z + d) % NZ) * NG + q, y) for d in range(1, NZ)]
    for peer in peers:
        pl.semaphore_signal(barrier, inc=1, device_id=peer, device_id_type=MESH)
    wt[z, x, core] = weight_ref[...]
    pl.semaphore_wait(barrier, len(peers))

    half = rows // 2

    def gblock(c, t):
        t = (t + NY) % NY
        return gg.at[pl.ds(c * half, half), pl.ds(pl.multiple_of(t * width, width), width)]

    def gstep(c, d):
        out = []
        own = grad_ref.at[pl.ds(c * half, half)]
        if d < 4 or c == 0:
            block = gblock(c, y - d + 1)
            out.append(push(own if d == 1 else block, block, i, yr))
        if d < 4 or c == 1:
            block = gblock(c, y + d - 1)
            out.append(push(own if d == 1 else block, block, i, yl))
        return out

    def arrived(cs):
        for c in cs:
            c.wait_recv()

    def ablock(c, zz):
        return wt.at[(zz + NZ) % NZ, pl.ds(2 * c, 2), core, pl.ds(0, 32), :]

    def bpiece(zz, xx, lo=32, n=32):
        return wt.at[(zz + NZ) % NZ, (xx + NX) % NX, core, pl.ds(lo, n), :]

    def bcolumn(xx):
        return wt.at[:, (xx + NX) % NX, core, pl.ds(32, 32), :]

    def same(block, dest):
        return push(block, block, dest, y)

    def astep(c, d):
        out = []
        if d < 4 or c == 0:
            out.append(same(ablock(c, z - d + 1), zr))
        if d < 4 or c == 1:
            out.append(same(ablock(c, z + d - 1), zl))
        return out

    def bstep(d):
        n = 32 if d < 4 else 16
        lo = 32 if d < 4 else 48
        return [same(bpiece(z - d + 1, x, 32, n), zr), same(bpiece(z + d - 1, x, lo, n), zl)]

    def xstep(p):
        out = []
        for zz in [z + p] if p in (0, 4) else [z + p, z - p]:
            out += [same(bpiece(zz, x), xr), same(bpiece(zz, x), xl)]
        return out

    flight = {"X": []}
    mates = []
    own = wt.at[z, x, core, pl.ds(0, 32), :]
    flight["g01"] = gstep(0, 1)
    flight["a0"] = [same(own, at(z, x + d, core)) for d in range(1, NX)]
    flight["b1"] = bstep(1)
    flight["x0"] = xstep(0)
    flight["g11"] = gstep(1, 1)

    get_streams.wait()

    def widen(cg, _):
        lanes = pl.ds(pl.multiple_of(cg * LANES, LANES), LANES)
        for s in range(3):
            u32[s, cg, 8 : 8 + rows, :] = sv[s, :, lanes].astype(jnp.float32)
            tail[s, cg] = u32[s, cg, pl.ds(jnp.clip(count, 8, rows), 8), :]
        return 0

    lax.fori_loop(0, groups, widen, 0)
    tails = push(tail, halo, up, y)

    def forward(cg):
        lanes = pl.ds(pl.multiple_of(cg * LANES, LANES), LANES)
        coef = []
        for s in range(3):
            u32[s, cg, 0:8, :] = jnp.where(i > 0, halo[s, cg], 0.0)
            du32[s, cg, 0:TILE, :] = jnp.zeros((TILE, LANES), jnp.float32)
            du32[s, cg, TILE + rows :, :] = jnp.zeros((TILE, LANES), jnp.float32)
            dc32[s, cg, rows:, :] = jnp.zeros((8, LANES), jnp.float32)
            zbuf[s, cg] = jnp.zeros((24, LANES), jnp.float32)
            coef.append([filters_ref[s, pl.ds(j, 1), lanes] for j in range(taps)])

        def chunk(r, _):
            r0 = pl.multiple_of(r * CH, CH)
            c = []
            for s in range(3):
                acc = coef[s][0] * u32[s, cg, pl.ds(8 + r0, CH), :]
                for j in range(1, taps):
                    acc = acc + coef[s][j] * u32[s, cg, pl.ds(8 + r0 - j, CH), :]
                c.append(acc)
            prod[0, cg, pl.ds(r0, CH), :] = c[1] * c[2]
            prod[1, cg, pl.ds(r0, CH), :] = c[0] * c[2]
            prod[2, cg, pl.ds(r0, CH), :] = c[0] * c[1]
            return 0

        lax.fori_loop(0, rows // CH, chunk, 0)

    done = 0
    for token in ORDER:
        kind = token[0]
        if kind == "f":
            if done == 0:
                tails.wait_recv()
            forward(done)
            done += 1
            continue
        arrived(flight[token])
        if kind == "g" or kind == "A":
            c, d = int(token[1]), int(token[2])
            if d < 4:
                flight[f"{kind}{c}{d + 1}"] = (gstep if kind == "g" else astep)(c, d + 1)
            if kind == "A":
                mates.append(same(ablock(c, z - d), mate))
                if d < 4:
                    mates.append(same(ablock(c, z + d), mate))
        elif kind == "a":
            flight["A01"], flight["A11"] = astep(0, 1), astep(1, 1)
            mates += [same(ablock(0, z), mate), same(ablock(1, z), mate)]
        elif kind == "b":
            d = int(token[1])
            if d < 4:
                flight[f"b{d + 1}"] = bstep(d + 1)
            else:
                mates.append(same(bcolumn(x), mate))
            flight[f"x{d}"] = xstep(d)
        elif kind == "x":
            p = int(token[1])
            if p < 4:
                flight["X"].append(same(bpiece(z + p, x - 1), xr))
            if p > 0:
                flight["X"].append(same(bpiece(z - p, x + 1), xl))
            if p == 4:
                mates += [same(bcolumn(x - 1), mate), same(bcolumn(x + 1), mate)]
        else:
            mates.append(same(bcolumn(x + 2), mate))
    get_grad.wait()
    arrived(mates)

    def project(c):
        def block(n, _):
            cols = pl.ds(pl.multiple_of(n * 256, 256), 256)
            w = wt[:, :, :, :, cols].reshape(NZ * NG * 64, 256)
            dy = jnp.dot(gg[pl.ds(c * half, half), :], w, preferred_element_type=jnp.float32)
            for r in range(c * half, (c + 1) * half, CH):
                live = lax.broadcasted_iota(jnp.int32, (CH, LANES), 0) + r < count
                for e in range(2):
                    part = dy[r - c * half : r - c * half + CH, e * LANES : (e + 1) * LANES]
                    part = part.astype(jnp.bfloat16).astype(jnp.float32)
                    for s in range(3):
                        dc = jnp.where(live, part * prod[s, 2 * n + e, r : r + CH, :], 0.0)
                        dc32[s, 2 * n + e, r : r + CH, :] = dc.astype(jnp.bfloat16).astype(jnp.float32)
            return 0

        lax.fori_loop(0, groups // 2, block, 0)

    def correlate(c):
        def group(cg, _):
            for s in range(3):
                acc = [jnp.zeros((8, LANES), jnp.float32)] * taps
                for r in range(c * half, (c + 1) * half, CH):
                    dc = dc32[s, cg, r : r + CH, :]
                    for j in range(taps):
                        term = dc * u32[s, cg, 8 + r - j : 8 + r - j + CH, :]
                        acc[j] = acc[j] + term.reshape(CH // 8, 8, LANES).sum(0)
                if c == 0:
                    fsc[cg, s] = jnp.zeros((8, LANES), jnp.float32)
                for j in range(taps):
                    term = acc[j].sum(0, keepdims=True)
                    if c == 1:
                        term = term + fsc[cg, s, j : j + 1, :]
                    fsc[cg, s, j : j + 1, :] = term
            return 0

        lax.fori_loop(0, groups, group, 0)

    arrived(flight["g04"])
    project(0)
    head[...] = dc32[:, :, 0:8, :]
    heads = push(head, heads_in, down, y)
    correlate(0)
    arrived(flight["g14"])
    project(1)
    correlate(1)
    f1 = []
    for d in range(1, NG):
        to = (q + d) % NG
        f1.append(push(fsc.at[to], p1.at[d], z * NG + to, y))

    heads.wait_recv()

    def backward(cg, _):
        lanes = pl.ds(pl.multiple_of(cg * LANES, LANES), LANES)
        for s in range(3):
            zbuf[s, cg, 8:16, :] = jnp.where(i < n_ctx - 1, heads_in[s, cg], 0.0)

        def insert(r, _):
            r0 = pl.multiple_of(r * 8, 8)
            at_row = jnp.clip(r0 - count, -8, 8) + 8
            for s in range(3):
                dc32[s, cg, pl.ds(r0, 8), :] += zbuf[s, cg, pl.ds(at_row, 8), :]
            return 0

        lax.fori_loop(rows // 16, rows // 8 + 1, insert, 0)
        coef = [[filters_ref[s, pl.ds(j, 1), lanes] for j in range(taps)] for s in range(3)]

        for r in range(0, rows, CH):
            live = lax.broadcasted_iota(jnp.int32, (CH, LANES), 0) + r < count
            for s in range(3):
                acc = coef[s][0] * dc32[s, cg, r : r + CH, :]
                for j in range(1, taps):
                    acc = acc + coef[s][j] * dc32[s, cg, r + j : r + j + CH, :]
                du32[s, cg, TILE + r : TILE + r + CH, :] = jnp.where(live, acc, 0.0)

        for s in range(3):
            for k in range(SLOTS):
                block = jnp.abs(du32[s, cg, pl.ds((k + 1) * TILE - offset, TILE), :])
                top = block.reshape(TILE // 8, 8, LANES).max(0).max(0, keepdims=True)
                msc[k, pl.ds(s * groups + cg, 1), :] = top
        return 0

    lax.fori_loop(0, groups // 2, backward, 0)
    arrived(f1)
    part = fsc[q]
    for d in range(1, NG):
        part = part + p1[d]
    p2[z] = part
    f2 = []
    for d in range(1, NZ):
        f2.append(push(p2.at[z], p2.at[z], ((z + d) % NZ) * NG + q, y))
    lax.fori_loop(groups // 2, groups, backward, 0)
    tmx[...] = msc[last_slot]
    to_next = push(tmx, max_prev, up, y)
    to_prev = push(msc.at[0], max_next, down, y)

    arrived(f2)
    total = p2[0]
    for d in range(1, NZ):
        total = total + p2[d]
    fgrad_ref[q] = total
    f3 = []
    for d in range(1, NG):
        f3.append(push(fgrad_ref.at[q], fgrad_ref.at[q], z * NG + (q + d) % NG, y))

    to_next.wait_recv()
    to_prev.wait_recv()
    prev = jnp.where(offset != 0, max_prev[...], 0.0)
    follow = jnp.where((first + count) % TILE != 0, max_next[...], 0.0)
    for k in range(SLOTS):
        top = msc[k]
        if k == 0:
            top = jnp.maximum(top, prev)
        top = jnp.maximum(top, jnp.where(last_slot == k, follow, 0.0))
        scale = top + 1e-6
        inv_ref[k] = 1.0 / scale
        scales_ref[k] = jnp.where(last_slot >= k, scale, 0.0)

    arrived(f3)
    for c in copies:
        c.wait_send()


def finish(starts_ref, du_ref, inv_ref, scale_ref, fgrad_ref, pay_out, scales_out, fgrad_out):
    s = pl.program_id(0)
    groups, rows = du_ref.shape[1], pay_out.shape[1]
    offset = starts_ref[0] % TILE
    taps = fgrad_out.shape[1]

    def group(cg, _):
        lanes = pl.ds(pl.multiple_of(cg * LANES, LANES), LANES)
        row = pl.ds(s * groups + cg, 1)
        inv = [inv_ref[k, row, :] for k in range(SLOTS)]
        for k in range(SLOTS):
            scales_out[0, k : k + 1, lanes] = scale_ref[k, row, :]
        fgrad_out[0, :, lanes] = fgrad_ref[cg, s, :taps, :]
        for r in range(0, rows, CH):
            pos = lax.broadcasted_iota(jnp.int32, (CH, LANES), 0) + (r + offset)
            scale = jnp.where(pos >= 3 * TILE, inv[3], inv[2])
            scale = jnp.where(pos >= 2 * TILE, scale, inv[1])
            scale = jnp.where(pos >= TILE, scale, inv[0])
            du = du_ref[s, cg, TILE + r : TILE + r + CH, :]
            pay_out[0, r : r + CH, lanes] = (du * scale).astype(jnp.bfloat16)
        return 0

    lax.fori_loop(0, groups, group, 0)


def shards(streams, filters, out_weight, grad_out, counts, starts):
    _, rows, channels = streams.shape
    taps = filters.shape[1]
    width = grad_out.shape[1]
    g = channels // LANES
    vmem = pl.BlockSpec(memory_space=pltpu.VMEM)
    anywhere = pl.BlockSpec(memory_space=pl.ANY)
    smem = pl.BlockSpec(memory_space=pltpu.SMEM)
    f32, bf16 = jnp.float32, jnp.bfloat16
    V = pltpu.VMEM
    du, inv, scale, fgrad = pl.pallas_call(
        kernel,
        out_shape=(
            V((3, g, rows + 2 * TILE, LANES), f32),
            V((SLOTS, 3 * g, LANES), f32),
            V((SLOTS, 3 * g, LANES), f32),
            V((NG, 3, 8, LANES), f32),
        ),
        in_specs=[anywhere, vmem, vmem, anywhere, smem, smem],
        out_specs=(vmem, vmem, vmem, vmem),
        scratch_shapes=[
            V((3, rows, channels), bf16),
            V((3, g, rows + 8, LANES), f32),
            V((3, g, rows, LANES), f32),
            V((NZ, NX, NC, 64, channels), bf16),
            V((rows, NY * width), bf16),
            V((3, g, rows + 8, LANES), f32),
            V((3, g, 8, LANES), f32),
            V((3, g, 8, LANES), f32),
            V((3, g, 8, LANES), f32),
            V((3, g, 8, LANES), f32),
            V((3, g, 24, LANES), f32),
            V((SLOTS, 3 * g, LANES), f32),
            V((3 * g, LANES), f32),
            V((3 * g, LANES), f32),
            V((3 * g, LANES), f32),
            V((g, 3, 8, LANES), f32),
            V((NG, 3, 8, LANES), f32),
            V((NZ, 3, 8, LANES), f32),
            pltpu.SemaphoreType.DMA((128,)),
            pltpu.SemaphoreType.DMA((128,)),
            pltpu.SemaphoreType.DMA((2,)),
        ],
        compiler_params=pltpu.CompilerParams(
            collective_id=0, has_side_effects=True, vmem_limit_bytes=VLIM * 1024 * 1024
        ),
        cost_estimate=pl.CostEstimate(
            flops=2 * rows * channels * NY * width, bytes_accessed=12 * rows * channels, transcendentals=0
        ),
    )(streams, filters, out_weight.T, grad_out, counts, starts)
    return pl.pallas_call(
        finish,
        grid=(3,),
        out_shape=(
            jax.ShapeDtypeStruct((3, rows, channels), bf16),
            jax.ShapeDtypeStruct((3, SLOTS, channels), f32),
            jax.ShapeDtypeStruct((3, taps, channels), f32),
        ),
        in_specs=[smem, vmem, vmem, vmem, vmem],
        out_specs=(
            pl.BlockSpec((1, rows, channels), lambda s: (s, 0, 0)),
            pl.BlockSpec((1, SLOTS, channels), lambda s: (s, 0, 0)),
            pl.BlockSpec((1, taps, channels), lambda s: (s, 0, 0)),
        ),
        compiler_params=pltpu.CompilerParams(vmem_limit_bytes=20 * 1024 * 1024),
    )(starts, du, inv, scale, fgrad)


def solution(mesh):
    return jax.shard_map(
        shards,
        mesh=mesh,
        in_specs=(
            P(None, "ctx", "tp"),
            P(None, None, "tp"),
            P("tp", "ctx"),
            P("ctx", "tp"),
            P("ctx"),
            P("ctx"),
        ),
        out_specs=(P(None, "ctx", "tp"), P(None, "ctx", "tp"), P(None, None, "tp")),
        check_vma=False,
    )
```

time: 91.8 us -> 79.1 us (0.86)
  Pallas kernels: 83.3 us -> 74.1 us
  local copies, waits for them, and re-layouts: 6.32 us -> 2.78 us
    pallas_call x1 -> x2, Pallas kernels: 83.3 us -> 74.1 us  [the longest x1 71.3 us: shards(): pl.pallas_call(kernel, out_shape=(V((3, g, rows + 2 * TILE, LANES), f32),...]
    unnamed x8 -> x6, local copies, waits for them, and re-layouts: 6.32 us -> 2.78 us
where the time goes in v2:
time: 79.1 us; the launch traced here: 78.9 us
  Pallas kernels  74.1 us (94%)
  local copies, waits for them, and re-layouts  2.78 us (4%)
  between operations  1.94 us (2%)
    pallas_call x1, Pallas kernels, shards(): pl.pallas_call(kernel, out_shape=(V((3, g, rows + 2 * TILE, LANES), f32),...  71.3 us
    pallas_call x1, Pallas kernels, shards(): pl.pallas_call(finish, grid=(3,), out_shape=(jax.ShapeDtypeStruct((3, row...  2.86 us
    unnamed x6, local copies, waits for them, and re-layouts  2.78 us

profile of v2, /device:TPU:1, one launch (start us, length us, event | category | flops | bytes accessed | tf_op | source)
XLA Modules:
  0.0 78.9 jit_solution(6134705548605959824)
XLA Ops:
  1.9 0.0 copy-start
  1.9 1.0 %copy-done = bf16[384,512]{1,0:T(8,128)(2,1)S(1)} copy-done((bf16[384,512]{1,0:T(8,128)(2,1)S(1)}, bf16[384,512]{1,0:T(8,128)(2,1)}, u32[]{:S(2)}) %copy-start) | copy-done | bytes 393240
  2.9 0.0 copy-start.1
  2.9 0.9 %copy-done.1 = bf16[1024,64]{0,1:T(8,128)(2,1)S(1)} copy-done((bf16[1024,64]{0,1:T(8,128)(2,1)S(1)}, bf16[1024,64]{0,1:T(8,128)(2,1)}, u32[]{:S(2)}) %copy-start.1) | copy-done | bytes 131096
  3.8 0.0 copy-start.2
  3.8 0.9 %copy-done.2 = f32[3,7,1024]{2,1,0:T(8,128)S(1)} copy-done((f32[3,7,1024]{2,1,0:T(8,128)S(1)}, f32[3,7,1024]{2,1,0:T(8,128)}, u32[]{:S(2)}) %copy-start.2) | copy-done | bytes 86040
  4.7 71.3 %shard_map.85 = (f32[3,8,640,128]{3,2,1,0:T(8,128)S(1)}, f32[4,24,128]{2,1,0:T(8,128)S(1)}, f32[4,24,128]{2,1,0:T(8,128)S(1)}, f32[8,3,8,128]{3,2,1,0:T(8,128)S(1)}) custom-call(bf16[3,384,1024]{2,1,0:T(8,128)(2,1)} %streams_ref.1, f32[3,7,1024]{2,1,0:T(8,128)S(1)} %copy-done.2, bf16[64,1024]{1,0:T(8,128)(2,1)S(1)} %bitcast.1, bf16[384,512]{1,0:T(8,128)(2,1)S(1)} %copy-done, ...), custom_call_target="tpu_custom_call" | custom-call | flops 3221225472 | bytes 4718592 | tf_op jit(solution)/shard_map/pallas_call | solution.py:385
  76.0 2.9 %shard_map.86 = (bf16[3,384,1024]{2,1,0:T(8,128)(2,1)}, f32[3,4,1024]{2,1,0:T(4,128)}, f32[3,7,1024]{2,1,0:T(8,128)}) custom-call(s32[1]{0:T(128)S(6)} %copy.10.starts_ref, f32[3,8,640,128]{3,2,1,0:T(8,128)S(1)} %get-tuple-element.7.du_ref, f32[4,24,128]{2,1,0:T(8,128)S(1)} %get-tuple-element.8.inv_ref, f32[4,24,128]{2,1,0:T(8,128)S(1)} %get-tuple-element.9.scale_ref, ...), custom_call_target="tpu_custom_call" | custom-call | tf_op jit(solution)/shard_map/pallas_call | solution.py:425
Async XLA Ops:
  1.9 1.0 %copy-start = (bf16[384,512]{1,0:T(8,128)(2,1)S(1)}, bf16[384,512]{1,0:T(8,128)(2,1)}, u32[]{:S(2)}) copy-start(bf16[384,512]{1,0:T(8,128)(2,1)} %grad_ref.1) | copy-start | bytes 1179652
  2.9 0.9 %copy-start.1 = (bf16[1024,64]{0,1:T(8,128)(2,1)S(1)}, bf16[1024,64]{0,1:T(8,128)(2,1)}, u32[]{:S(2)}) copy-start(bf16[1024,64]{0,1:T(8,128)(2,1)} %param.8) | copy-start | bytes 393220
  3.8 0.9 %copy-start.2 = (f32[3,7,1024]{2,1,0:T(8,128)S(1)}, f32[3,7,1024]{2,1,0:T(8,128)}, u32[]{:S(2)}) copy-start(f32[3,7,1024]{2,1,0:T(8,128)} %filters_ref.1) | copy-start | bytes 258052

commit v3 on v2

v3 whole, which is shorter than its diff:
```python
import functools

import jax
import jax.numpy as jnp
from jax import lax
from jax.experimental import pallas as pl
from jax.experimental.pallas import tpu as pltpu
from jax.sharding import PartitionSpec as P

MESH = pl.DeviceIdType.MESH
TILE = 128
LANES = 128
NZ, NX, NC, NY = 8, 4, 2, 8
NG = NX * NC
CH = 64
SLOTS = 4
VLIM = 54


ORDER = (
    "b01", "g001", "a0", "b02", "f", "x00", "f", "f", "f", "g011", "x01", "f", "f", "f", "x02",
    "f", "A01", "g002", "b03", "g012", "x03", "A02", "b04", "g003", "b11", "a1", "x10", "g013",
    "x04", "A03", "b12", "g004", "x11", "X0", "g014", "g101", "x12", "A11", "A04", "g111", "b13",
    "P0", "g102", "x13", "A12", "P1", "b14", "g112", "x14", "g103", "A13", "X1", "Q0", "g113",
    "A14", "P2", "P3", "Q1",
)


def kernel(
    streams_ref, filters_ref, weight_ref, grad_ref, counts_ref, starts_ref,
    du32, inv_ref, scales_ref, fgrad_ref,
    sv, fv, u32, prod, wt, gg, dyb, dc32, tail, halo, head, heads_in, zbuf,
    msc, tmx, max_prev, max_next, facc, fsc, p1, p2,
    send, recv, local,
):
    rows = grad_ref.shape[0]
    width = grad_ref.shape[1]
    taps = filters_ref.shape[1]
    groups = weight_ref.shape[1] // LANES
    i = lax.axis_index("ctx")
    y = lax.axis_index("tp")
    z = i // NG
    q = i % NG
    x = q // NC
    core = q % NC
    n_ctx = NZ * NG

    count = counts_ref[0]
    first = starts_ref[0]
    offset = first % TILE
    last_slot = jnp.clip((offset + count - 1) // TILE, 0, SLOTS - 1)

    def at(zz, xx, cc):
        return ((zz + NZ) % NZ) * NG + ((xx + NX) % NX) * NC + cc

    copies = []

    def push(src, dst, ctx, tp):
        k = len(copies)
        c = pltpu.make_async_remote_copy(
            src_ref=src, dst_ref=dst, send_sem=send.at[k], recv_sem=recv.at[k],
            device_id=(ctx, tp), device_id_type=MESH,
        )
        c.start()
        copies.append(c)
        return c

    up, down = (i + 1) % n_ctx, (i + n_ctx - 1) % n_ctx
    yr, yl = (y + 1) % NY, (y + NY - 1) % NY
    zr, zl = at(z + 1, x, core), at(z - 1, x, core)
    xr, xl = at(z, x + 1, core), at(z, x - 1, core)
    mate = at(z, x, 1 - core)

    get_streams = pltpu.make_async_copy(streams_ref, sv, local.at[0])
    get_streams.start()
    own_cols = pl.ds(pl.multiple_of(y * width, width), width)
    get_grad = pltpu.make_async_copy(grad_ref, gg.at[:, own_cols], local.at[1])
    get_grad.start()

    get_weight = pltpu.make_async_copy(weight_ref, wt.at[z, x, core], local.at[2])
    get_weight.start()
    get_filters = pltpu.make_async_copy(filters_ref, fv, local.at[3])
    get_filters.start()

    barrier = pltpu.get_barrier_semaphore()
    peers = [(i, yr), (i, yl), (up, y), (down, y)]
    peers += [(z * NG + (q + d) % NG, y) for d in range(1, NG)]
    peers += [(((z + d) % NZ) * NG + q, y) for d in range(1, NZ)]
    for peer in peers:
        pl.semaphore_signal(barrier, inc=1, device_id=peer, device_id_type=MESH)
    pl.semaphore_wait(barrier, len(peers))

    half = rows // 2
    quarter = half // 2

    def gblock(c, u, t):
        t = (t + NY) % NY
        cols = pl.ds(pl.multiple_of(t * width, width), width)
        return gg.at[pl.ds(c * half + u * quarter, quarter), cols]

    def gstep(c, u, d):
        out = []
        own = grad_ref.at[pl.ds(c * half + u * quarter, quarter)]
        if d < 4 or u == 0:
            block = gblock(c, u, y - d + 1)
            out.append(push(own if d == 1 else block, block, i, yr))
        if d < 4 or u == 1:
            block = gblock(c, u, y + d - 1)
            out.append(push(own if d == 1 else block, block, i, yl))
        return out

    def arrived(cs):
        for c in cs:
            c.wait_recv()

    span = groups * LANES // 2

    def ablock(n, zz, lo=0, many=NX):
        return wt.at[(zz + NZ) % NZ, pl.ds(lo, many), core, pl.ds(0, 32), pl.ds(n * span, span)]

    def bpiece(n, zz, xx, lo=32, many=32):
        return wt.at[(zz + NZ) % NZ, (xx + NX) % NX, core, pl.ds(lo, many), pl.ds(n * span, span)]

    def bcolumn(n, xx):
        return wt.at[:, (xx + NX) % NX, core, pl.ds(32, 32), pl.ds(n * span, span)]

    def same(block, dest):
        return push(block, block, dest, y)

    def astep(n, d):
        many = NX if d < 4 else NX // 2
        lo = NX - many
        return [same(ablock(n, z - d + 1, 0, many), zr), same(ablock(n, z + d - 1, lo, many), zl)]

    def bstep(n, d):
        many = 32 if d < 4 else 16
        lo = 64 - many
        return [same(bpiece(n, z - d + 1, x, 32, many), zr), same(bpiece(n, z + d - 1, x, lo, many), zl)]

    def xstep(n, p):
        out = []
        for zz in [z + p] if p in (0, 4) else [z + p, z - p]:
            out += [same(bpiece(n, zz, x), xr), same(bpiece(n, zz, x), xl)]
        return out

    def wstart(n):
        own = wt.at[z, x, core, pl.ds(0, 32), pl.ds(n * span, span)]
        flight[f"a{n}"] = [same(own, at(z, x + d, core)) for d in range(1, NX)]
        flight[f"b{n}1"] = bstep(n, 1)
        flight[f"x{n}0"] = xstep(n, 0)

    flight = {"X0": [], "X1": []}
    mates = [[], []]
    flight["g001"] = gstep(0, 0, 1)
    get_weight.wait()
    wstart(0)
    flight["g011"] = gstep(0, 1, 1)

    get_streams.wait()

    def widen(cg, _):
        lanes = pl.ds(pl.multiple_of(cg * LANES, LANES), LANES)
        for s in range(3):
            u32[s, cg, 8 : 8 + rows, :] = sv[s, :, lanes].astype(jnp.float32)
            tail[s, cg] = u32[s, cg, pl.ds(jnp.clip(count, 8, rows), 8), :]
        return 0

    lax.fori_loop(0, groups, widen, 0)
    tails = push(tail, halo, up, y)

    def forward(cg):
        lanes = pl.ds(pl.multiple_of(cg * LANES, LANES), LANES)
        coef = []
        for s in range(3):
            u32[s, cg, 0:8, :] = jnp.where(i > 0, halo[s, cg], 0.0)
            du32[s, cg, 0:TILE, :] = jnp.zeros((TILE, LANES), jnp.float32)
            du32[s, cg, TILE + rows :, :] = jnp.zeros((TILE, LANES), jnp.float32)
            dc32[s, cg, rows:, :] = jnp.zeros((8, LANES), jnp.float32)
            zbuf[s, cg] = jnp.zeros((24, LANES), jnp.float32)
            for k in range(taps, 8):
                fsc[cg, s, k : k + 1, :] = jnp.zeros((1, LANES), jnp.float32)
            coef.append([fv[s, pl.ds(j, 1), lanes] for j in range(taps)])

        def chunk(r, _):
            r0 = pl.multiple_of(r * CH, CH)
            c = []
            for s in range(3):
                acc = coef[s][0] * u32[s, cg, pl.ds(8 + r0, CH), :]
                for j in range(1, taps):
                    acc = acc + coef[s][j] * u32[s, cg, pl.ds(8 + r0 - j, CH), :]
                c.append(acc)
            prod[0, cg, pl.ds(r0, CH), :] = c[1] * c[2]
            prod[1, cg, pl.ds(r0, CH), :] = c[0] * c[2]
            prod[2, cg, pl.ds(r0, CH), :] = c[0] * c[1]
            return 0

        lax.fori_loop(0, rows // CH, chunk, 0)

    def project(c, b, slot):
        cols = pl.ds(pl.multiple_of(b * 256, 256), 256)
        w = wt[:, :, :, :, cols].reshape(NZ * NG * 64, 256)
        dy = jnp.dot(gg[pl.ds(c * half, half), :], w, preferred_element_type=jnp.float32)
        dyb[slot] = dy.astype(jnp.bfloat16).astype(jnp.float32)

    def gate(c, b, slot):
        for r in range(c * half, (c + 1) * half, CH):
            live = lax.broadcasted_iota(jnp.int32, (CH, LANES), 0) + r < count
            for e in range(2):
                dy = dyb[slot, r - c * half : r - c * half + CH, e * LANES : (e + 1) * LANES]
                for s in range(3):
                    dc = jnp.where(live, dy * prod[s, 2 * b + e, r : r + CH, :], 0.0)
                    dc32[s, 2 * b + e, r : r + CH, :] = dc.astype(jnp.bfloat16).astype(jnp.float32)
        for e in range(2):
            cg = 2 * b + e
            for s in range(3):
                if c == 0:
                    acc = [jnp.zeros((8, LANES), jnp.float32)] * taps
                    head[s, cg] = dc32[s, cg, 0:8, :]
                else:
                    acc = [facc[cg, s, j] for j in range(taps)]
                for r in range(c * half, (c + 1) * half, CH):
                    dc = dc32[s, cg, r : r + CH, :]
                    for j in range(taps):
                        term = dc * u32[s, cg, 8 + r - j : 8 + r - j + CH, :]
                        acc[j] = acc[j] + term.reshape(CH // 8, 8, LANES).sum(0)
                for j in range(taps):
                    if c == 0:
                        facc[cg, s, j] = acc[j]
                    else:
                        fsc[cg, s, j : j + 1, :] = acc[j].sum(0, keepdims=True)

    def rows_back(cg, lo, hi):
        lanes = pl.ds(pl.multiple_of(cg * LANES, LANES), LANES)
        coef = [[fv[s, pl.ds(j, 1), lanes] for j in range(taps)] for s in range(3)]
        for r in range(lo, hi, CH):
            live = lax.broadcasted_iota(jnp.int32, (CH, LANES), 0) + r < count
            for s in range(3):
                acc = coef[s][0] * dc32[s, cg, r : r + CH, :]
                for j in range(1, taps):
                    acc = acc + coef[s][j] * dc32[s, cg, r + j : r + j + CH, :]
                du32[s, cg, TILE + r : TILE + r + CH, :] = jnp.where(live, acc, 0.0)

    early = (half - 8) // CH * CH

    def first_rows(cg, _):
        rows_back(cg, 0, early)
        return 0

    done = 0
    for token in ORDER:
        kind = token[0]
        if kind == "f":
            if done == 0:
                get_filters.wait()
                tails.wait_recv()
            forward(done)
            done += 1
            continue
        n = int(token[1])
        if kind == "P":
            if n == 0:
                get_grad.wait()
            if n % 2 == 0:
                arrived(mates[n // 2])
            project(0, n, 0)
            gate(0, n, 0)
            continue
        if kind == "Q":
            lax.fori_loop(n * groups // 2, (n + 1) * groups // 2, first_rows, 0)
            continue
        arrived(flight[token])
        if kind == "g":
            u, d = int(token[2]), int(token[3])
            if d < 4:
                flight[f"g{n}{u}{d + 1}"] = gstep(n, u, d + 1)
            if d == 3 and n == 0:
                flight[f"g1{u}1"] = gstep(1, u, 1)
        elif kind == "A":
            d = int(token[2])
            if d < 4:
                flight[f"A{n}{d + 1}"] = astep(n, d + 1)
                mates[n].append(same(ablock(n, z + d), mate))
            mates[n].append(same(ablock(n, z - d), mate))
        elif kind == "a":
            flight[f"A{n}1"] = astep(n, 1)
            mates[n].append(same(ablock(n, z), mate))
        elif kind == "b":
            d = int(token[2])
            if d < 4:
                flight[f"b{n}{d + 1}"] = bstep(n, d + 1)
            flight[f"x{n}{d}"] = xstep(n, d)
            if d == 4:
                mates[n].append(same(bcolumn(n, x), mate))
            if n == 0 and d == 3:
                wstart(1)
        elif kind == "x":
            p = int(token[2])
            if p < 4:
                flight[f"X{n}"].append(same(bpiece(n, z + p, x - 1), xr))
            if p > 0:
                flight[f"X{n}"].append(same(bpiece(n, z - p, x + 1), xl))
            if p == 4:
                mates[n] += [same(bcolumn(n, x - 1), mate), same(bcolumn(n, x + 1), mate)]
        else:
            mates[n].append(same(bcolumn(n, x + 2), mate))

    heads = push(head, heads_in, down, y)
    arrived(flight["g104"])
    arrived(flight["g114"])
    project(1, 0, 0)

    def both(b, _):
        gate(1, b - 1, (b - 1) % 2)
        project(1, b, b % 2)
        return 0

    lax.fori_loop(1, groups // 2, both, 0)
    gate(1, groups // 2 - 1, (groups // 2 - 1) % 2)
    f1 = []
    for d in range(1, NG):
        to = (q + d) % NG
        f1.append(push(fsc.at[to], p1.at[d], z * NG + to, y))

    heads.wait_recv()

    def backward(cg, _):
        for s in range(3):
            zbuf[s, cg, 8:16, :] = jnp.where(i < n_ctx - 1, heads_in[s, cg], 0.0)

        def insert(r, _):
            r0 = pl.multiple_of(r * 8, 8)
            at_row = jnp.clip(r0 - count, -8, 8) + 8
            for s in range(3):
                dc32[s, cg, pl.ds(r0, 8), :] += zbuf[s, cg, pl.ds(at_row, 8), :]
            return 0

        lax.fori_loop(half // 8, rows // 8 + 1, insert, 0)
        rows_back(cg, early, rows)

        for s in range(3):
            for k in range(SLOTS):
                block = jnp.abs(du32[s, cg, pl.ds((k + 1) * TILE - offset, TILE), :])
                top = block.reshape(TILE // 8, 8, LANES).max(0).max(0, keepdims=True)
                msc[k, pl.ds(s * groups + cg, 1), :] = top
        return 0

    lax.fori_loop(0, groups // 2, backward, 0)
    arrived(f1)
    part = fsc[q]
    for d in range(1, NG):
        part = part + p1[d]
    p2[z] = part
    f2 = []
    for d in range(1, NZ):
        f2.append(push(p2.at[z], p2.at[z], ((z + d) % NZ) * NG + q, y))
    lax.fori_loop(groups // 2, groups, backward, 0)
    tmx[...] = msc[last_slot]
    to_next = push(tmx, max_prev, up, y)
    to_prev = push(msc.at[0], max_next, down, y)

    arrived(f2)
    total = p2[0]
    for d in range(1, NZ):
        total = total + p2[d]
    fgrad_ref[q] = total
    f3 = []
    for d in range(1, NG):
        f3.append(push(fgrad_ref.at[q], fgrad_ref.at[q], z * NG + (q + d) % NG, y))

    to_next.wait_recv()
    to_prev.wait_recv()
    prev = jnp.where(offset != 0, max_prev[...], 0.0)
    follow = jnp.where((first + count) % TILE != 0, max_next[...], 0.0)
    for k in range(SLOTS):
        top = msc[k]
        if k == 0:
            top = jnp.maximum(top, prev)
        top = jnp.maximum(top, jnp.where(last_slot == k, follow, 0.0))
        scale = top + 1e-6
        inv_ref[k] = 1.0 / scale
        scales_ref[k] = jnp.where(last_slot >= k, scale, 0.0)

    arrived(f3)
    for c in copies:
        c.wait_send()


def finish(starts_ref, du_ref, inv_ref, scale_ref, fgrad_ref, pay_out, scales_out, fgrad_out):
    s = pl.program_id(0)
    groups, rows = du_ref.shape[1], pay_out.shape[1]
    base = pl.program_id(1) * rows
    offset = starts_ref[0] % TILE
    taps = fgrad_out.shape[1]

    def group(cg, _):
        lanes = pl.ds(pl.multiple_of(cg * LANES, LANES), LANES)
        row = pl.ds(s * groups + cg, 1)
        inv = [inv_ref[k, row, :] for k in range(SLOTS)]
        for k in range(SLOTS):
            scales_out[0, k : k + 1, lanes] = scale_ref[k, row, :]
        fgrad_out[0, :, lanes] = fgrad_ref[cg, s, :taps, :]
        for r in range(0, rows, CH):
            pos = lax.broadcasted_iota(jnp.int32, (CH, LANES), 0) + (base + r + offset)
            scale = jnp.where(pos >= 3 * TILE, inv[3], inv[2])
            scale = jnp.where(pos >= 2 * TILE, scale, inv[1])
            scale = jnp.where(pos >= TILE, scale, inv[0])
            du = du_ref[s, cg, pl.ds(pl.multiple_of(TILE + base + r, CH), CH), :]
            pay_out[0, r : r + CH, lanes] = (du * scale).astype(jnp.bfloat16)
        return 0

    lax.fori_loop(0, groups, group, 0)


def shards(streams, filters, out_weight, grad_out, counts, starts):
    _, rows, channels = streams.shape
    taps = filters.shape[1]
    width = grad_out.shape[1]
    g = channels // LANES
    vmem = pl.BlockSpec(memory_space=pltpu.VMEM)
    smem = pl.BlockSpec(memory_space=pltpu.SMEM)
    hbm = pl.BlockSpec(memory_space=pltpu.HBM)
    f32, bf16 = jnp.float32, jnp.bfloat16
    V = pltpu.VMEM
    du, inv, scale, fgrad = pl.pallas_call(
        kernel,
        out_shape=(
            V((3, g, rows + 2 * TILE, LANES), f32),
            V((SLOTS, 3 * g, LANES), f32),
            V((SLOTS, 3 * g, LANES), f32),
            V((NG, 3, 8, LANES), f32),
        ),
        in_specs=[hbm, hbm, hbm, hbm, smem, smem],
        out_specs=(vmem, vmem, vmem, vmem),
        scratch_shapes=[
            V((3, rows, channels), bf16),
            V((3, taps, channels), f32),
            V((3, g, rows + 8, LANES), f32),
            V((3, g, rows, LANES), f32),
            V((NZ, NX, NC, 64, channels), bf16),
            V((rows, NY * width), bf16),
            V((2, rows // 2, 256), f32),
            V((3, g, rows + 8, LANES), f32),
            V((3, g, 8, LANES), f32),
            V((3, g, 8, LANES), f32),
            V((3, g, 8, LANES), f32),
            V((3, g, 8, LANES), f32),
            V((3, g, 24, LANES), f32),
            V((SLOTS, 3 * g, LANES), f32),
            V((3 * g, LANES), f32),
            V((3 * g, LANES), f32),
            V((3 * g, LANES), f32),
            V((g, 3, 8, 8, LANES), f32),
            V((g, 3, 8, LANES), f32),
            V((NG, 3, 8, LANES), f32),
            V((NZ, 3, 8, LANES), f32),
            pltpu.SemaphoreType.DMA((176,)),
            pltpu.SemaphoreType.DMA((176,)),
            pltpu.SemaphoreType.DMA((4,)),
        ],
        compiler_params=pltpu.CompilerParams(
            collective_id=0, has_side_effects=True, vmem_limit_bytes=VLIM * 1024 * 1024
        ),
        cost_estimate=pl.CostEstimate(
            flops=2 * rows * channels * NY * width, bytes_accessed=12 * rows * channels, transcendentals=0
        ),
    )(streams, filters, out_weight.T, grad_out, counts, starts)
    return pl.pallas_call(
        finish,
        grid=(3, 2),
        out_shape=(
            jax.ShapeDtypeStruct((3, rows, channels), bf16),
            jax.ShapeDtypeStruct((3, SLOTS, channels), f32),
            jax.ShapeDtypeStruct((3, taps, channels), f32),
        ),
        in_specs=[smem, vmem, vmem, vmem, vmem],
        out_specs=(
            pl.BlockSpec((1, rows // 2, channels), lambda s, h: (s, h, 0)),
            pl.BlockSpec((1, SLOTS, channels), lambda s, h: (s, 0, 0)),
            pl.BlockSpec((1, taps, channels), lambda s, h: (s, 0, 0)),
        ),
        compiler_params=pltpu.CompilerParams(vmem_limit_bytes=20 * 1024 * 1024),
    )(starts, du, inv, scale, fgrad)


def solution(mesh):
    return jax.shard_map(
        shards,
        mesh=mesh,
        in_specs=(
            P(None, "ctx", "tp"),
            P(None, None, "tp"),
            P("tp", "ctx"),
            P("ctx", "tp"),
            P("ctx"),
            P("ctx"),
        ),
        out_specs=(P(None, "ctx", "tp"), P(None, "ctx", "tp"), P(None, None, "tp")),
        check_vma=False,
    )
```

time: 79.1 us -> 83.8 us (1.059)
  Pallas kernels: 74.1 us -> 81.6 us
  local copies, waits for them, and re-layouts: 2.78 us -> 0 us
    pallas_call x1, Pallas kernels: 71.3 us -> 78.1 us  [shards(): pl.pallas_call(kernel, out_shape=(V((3, g, rows + 2 * TILE, LANES), f32),...]
    unnamed x6 -> x0, local copies, waits for them, and re-layouts: 2.78 us -> none
where the time goes in v3:
time: 83.8 us; the launch traced here: 83.5 us
  Pallas kernels  81.6 us (97%)
  between operations  1.93 us (2%)
    pallas_call x1, Pallas kernels, shards(): pl.pallas_call(kernel, out_shape=(V((3, g, rows + 2 * TILE, LANES), f32),...  78.1 us
    pallas_call x1, Pallas kernels, shards(): pl.pallas_call(finish, grid=(3, 2), out_shape=(jax.ShapeDtypeStruct((3, r...  3.51 us

profile of v3, /device:TPU:1, one launch (start us, length us, event | category | flops | bytes accessed | tf_op | source)
XLA Modules:
  0.0 83.5 jit_solution(3950970718098741131)
XLA Ops:
  1.9 78.1 %shard_map.85 = (f32[3,8,640,128]{3,2,1,0:T(8,128)S(1)}, f32[4,24,128]{2,1,0:T(8,128)S(1)}, f32[4,24,128]{2,1,0:T(8,128)S(1)}, f32[8,3,8,128]{3,2,1,0:T(8,128)S(1)}) custom-call(bf16[3,384,1024]{2,1,0:T(8,128)(2,1)} %streams_ref.1, f32[3,7,1024]{2,1,0:T(8,128)} %filters_ref.1, bf16[64,1024]{1,0:T(8,128)(2,1)} %bitcast.1, bf16[384,512]{1,0:T(8,128)(2,1)} %grad_ref.1, ...), custom_call_target="tpu_custom_call" | custom-call | flops 3221225472 | bytes 4718592 | tf_op jit(solution)/shard_map/pallas_call | solution.py:424
  80.0 3.5 %shard_map.86 = (bf16[3,384,1024]{2,1,0:T(8,128)(2,1)}, f32[3,4,1024]{2,1,0:T(4,128)}, f32[3,7,1024]{2,1,0:T(8,128)}) custom-call(s32[1]{0:T(128)S(6)} %copy.10.starts_ref, f32[3,8,640,128]{3,2,1,0:T(8,128)S(1)} %get-tuple-element.7.du_ref, f32[4,24,128]{2,1,0:T(8,128)S(1)} %get-tuple-element.8.inv_ref, f32[4,24,128]{2,1,0:T(8,128)S(1)} %get-tuple-element.9.scale_ref, ...), custom_call_target="tpu_custom_call" | custom-call | tf_op jit(solution)/shard_map/pallas_call | solution.py:467

commit v4 on v2

--- a/solution.py
+++ b/solution.py
@@ -14,20 +14,19 @@
 NG = NX * NC
 CH = 64
 SLOTS = 4
-VLIM = 44
+VLIM = 54
 
 
 ORDER = (
-    "b1", "f", "b2", "a0", "g01", "f", "f", "f", "x0", "f", "b3", "f", "g11", "x1", "A01", "x2",
-    "A11", "f", "b4", "g02", "f", "A02", "x3", "g12", "A12", "x4", "A03", "g03", "X", "A13", "g13",
-    "A04", "A14",
+    "b1", "b2", "g01", "a0", "b3", "b4", "f", "g11", "f", "f", "A01", "f", "g02", "A11", "x0",
+    "A02", "g12", "A12", "x1", "g03", "A03", "A13", "g13", "X", "A04", "A14",
 )
 
 
 def kernel(
     streams_ref, filters_ref, weight_ref, grad_ref, counts_ref, starts_ref,
     du32, inv_ref, scales_ref, fgrad_ref,
-    sv, u32, prod, wt, gg, dc32, tail, halo, head, heads_in, zbuf,
+    sv, fv, u32, prod, wt, gg, dyb, dc32, tail, halo, head, heads_in, zbuf,
     msc, tmx, max_prev, max_next, fsc, p1, p2,
     send, recv, local,
 ):
@@ -75,13 +74,17 @@
     get_grad = pltpu.make_async_copy(grad_ref, gg.at[:, own_cols], local.at[1])
     get_grad.start()
 
+    get_weight = pltpu.make_async_copy(weight_ref, wt.at[z, x, core], local.at[2])
+    get_weight.start()
+    get_filters = pltpu.make_async_copy(filters_ref, fv, local.at[3])
+    get_filters.start()
+
     barrier = pltpu.get_barrier_semaphore()
     peers = [(i, yr), (i, yl), (up, y), (down, y)]
     peers += [(z * NG + (q + d) % NG, y) for d in range(1, NG)]
     peers += [(((z + d) % NZ) * NG + q, y) for d in range(1, NZ)]
     for peer in peers:
         pl.semaphore_signal(barrier, inc=1, device_id=peer, device_id_type=MESH)
-    wt[z, x, core] = weight_ref[...]
     pl.semaphore_wait(barrier, len(peers))
 
     half = rows // 2
@@ -105,14 +108,14 @@
         for c in cs:
             c.wait_recv()
 
-    def ablock(c, zz):
-        return wt.at[(zz + NZ) % NZ, pl.ds(2 * c, 2), core, pl.ds(0, 32), :]
-
-    def bpiece(zz, xx, lo=32, n=32):
-        return wt.at[(zz + NZ) % NZ, (xx + NX) % NX, core, pl.ds(lo, n), :]
-
-    def bcolumn(xx):
-        return wt.at[:, (xx + NX) % NX, core, pl.ds(32, 32), :]
+    def ablock(c, zz, many=2):
+        return wt.at[(zz + NZ) % NZ, pl.ds(2 * c, many), core, pl.ds(0, 32), :]
+
+    def bpiece(zz, lo=32, many=32):
+        return wt.at[(zz + NZ) % NZ, x, core, pl.ds(lo, many), :]
+
+    def bcolumn(xx, lo=0, many=NZ):
+        return wt.at[pl.ds(lo, many), (xx + NX) % NX, core, pl.ds(32, 32), :]
 
     def same(block, dest):
         return push(block, block, dest, y)
@@ -126,23 +129,20 @@
         return out
 
     def bstep(d):
-        n = 32 if d < 4 else 16
-        lo = 32 if d < 4 else 48
-        return [same(bpiece(z - d + 1, x, 32, n), zr), same(bpiece(z + d - 1, x, lo, n), zl)]
-
-    def xstep(p):
-        out = []
-        for zz in [z + p] if p in (0, 4) else [z + p, z - p]:
-            out += [same(bpiece(zz, x), xr), same(bpiece(zz, x), xl)]
-        return out
+        many = 32 if d < 4 else 16
+        return [same(bpiece(z - d + 1, 32, many), zr), same(bpiece(z + d - 1, 64 - many, many), zl)]
+
+    def xstep(h):
+        block = bcolumn(x, h * NZ // 2, NZ // 2)
+        return [same(block, xr), same(block, xl)]
 
     flight = {"X": []}
     mates = []
+    flight["g01"] = gstep(0, 1)
+    get_weight.wait()
+    flight["b1"] = bstep(1)
     own = wt.at[z, x, core, pl.ds(0, 32), :]
-    flight["g01"] = gstep(0, 1)
     flight["a0"] = [same(own, at(z, x + d, core)) for d in range(1, NX)]
-    flight["b1"] = bstep(1)
-    flight["x0"] = xstep(0)
     flight["g11"] = gstep(1, 1)
 
     get_streams.wait()
@@ -157,7 +157,7 @@
     lax.fori_loop(0, groups, widen, 0)
     tails = push(tail, halo, up, y)
 
-    def forward(cg):
+    def forward(cg, _):
         lanes = pl.ds(pl.multiple_of(cg * LANES, LANES), LANES)
         coef = []
         for s in range(3):
@@ -165,8 +165,10 @@
             du32[s, cg, 0:TILE, :] = jnp.zeros((TILE, LANES), jnp.float32)
             du32[s, cg, TILE + rows :, :] = jnp.zeros((TILE, LANES), jnp.float32)
             dc32[s, cg, rows:, :] = jnp.zeros((8, LANES), jnp.float32)
-            zbuf[s, cg] = jnp.zeros((24, LANES), jnp.float32)
-            coef.append([filters_ref[s, pl.ds(j, 1), lanes] for j in range(taps)])
+            zbuf[s, cg] = jnp.zeros((2 * CH + 8, LANES), jnp.float32)
+            for k in range(taps, 8):
+                fsc[cg, s, k : k + 1, :] = jnp.zeros((1, LANES), jnp.float32)
+            coef.append([fv[s, pl.ds(j, 1), lanes] for j in range(taps)])
 
         def chunk(r, _):
             r0 = pl.multiple_of(r * CH, CH)
@@ -182,93 +184,100 @@
             return 0
 
         lax.fori_loop(0, rows // CH, chunk, 0)
+        return 0
+
+    def project(b, slot):
+        cols = pl.ds(pl.multiple_of(b * 256, 256), 256)
+        w = wt[:, :, :, :, cols].reshape(NZ * NG * 64, 256)
+        dy = jnp.dot(gg[...], w, preferred_element_type=jnp.float32)
+        dyb[slot] = dy.astype(jnp.bfloat16).astype(jnp.float32)
+
+    def gate(b, slot):
+        for r in range(0, rows, CH):
+            live = lax.broadcasted_iota(jnp.int32, (CH, LANES), 0) + r < count
+            for e in range(2):
+                dy = dyb[slot, r : r + CH, e * LANES : (e + 1) * LANES]
+                for s in range(3):
+                    dc = jnp.where(live, dy * prod[s, 2 * b + e, r : r + CH, :], 0.0)
+                    dc32[s, 2 * b + e, r : r + CH, :] = dc.astype(jnp.bfloat16).astype(jnp.float32)
+        for e in range(2):
+            cg = 2 * b + e
+            for s in range(3):
+                acc = [jnp.zeros((8, LANES), jnp.float32)] * taps
+                head[s, cg] = dc32[s, cg, 0:8, :]
+                for r in range(0, rows, CH):
+                    dc = dc32[s, cg, r : r + CH, :]
+                    for j in range(taps):
+                        term = dc * u32[s, cg, 8 + r - j : 8 + r - j + CH, :]
+                        acc[j] = acc[j] + term.reshape(CH // 8, 8, LANES).sum(0)
+                for j in range(taps):
+                    fsc[cg, s, j : j + 1, :] = acc[j].sum(0, keepdims=True)
+
+    def rows_back(cg, lo, hi):
+        lanes = pl.ds(pl.multiple_of(cg * LANES, LANES), LANES)
+        coef = [[fv[s, pl.ds(j, 1), lanes] for j in range(taps)] for s in range(3)]
+        for r in range(lo, hi, CH):
+            live = lax.broadcasted_iota(jnp.int32, (CH, LANES), 0) + r < count
+            for s in range(3):
+                acc = coef[s][0] * dc32[s, cg, r : r + CH, :]
+                for j in range(1, taps):
+                    acc = acc + coef[s][j] * dc32[s, cg, r + j : r + j + CH, :]
+                du32[s, cg, TILE + r : TILE + r + CH, :] = jnp.where(live, acc, 0.0)
 
     done = 0
     for token in ORDER:
         kind = token[0]
         if kind == "f":
             if done == 0:
+                get_filters.wait()
                 tails.wait_recv()
-            forward(done)
-            done += 1
+            lax.fori_loop(done, done + groups // 4, forward, 0)
+            done += groups // 4
             continue
         arrived(flight[token])
         if kind == "g" or kind == "A":
             c, d = int(token[1]), int(token[2])
             if d < 4:
                 flight[f"{kind}{c}{d + 1}"] = (gstep if kind == "g" else astep)(c, d + 1)
-            if kind == "A":
-                mates.append(same(ablock(c, z - d), mate))
+            if kind == "A" and c == 1:
+                mates.append(same(ablock(0, z - d, NX), mate))
                 if d < 4:
-                    mates.append(same(ablock(c, z + d), mate))
+                    mates.append(same(ablock(0, z + d, NX), mate))
         elif kind == "a":
-            flight["A01"], flight["A11"] = astep(0, 1), astep(1, 1)
-            mates += [same(ablock(0, z), mate), same(ablock(1, z), mate)]
+            mates.append(same(ablock(0, z, NX), mate))
         elif kind == "b":
             d = int(token[1])
             if d < 4:
                 flight[f"b{d + 1}"] = bstep(d + 1)
-            else:
+            if d == 3:
+                flight["A01"], flight["A11"] = astep(0, 1), astep(1, 1)
+            if d == 4:
+                flight["x0"], flight["x1"] = xstep(0), xstep(1)
                 mates.append(same(bcolumn(x), mate))
-            flight[f"x{d}"] = xstep(d)
-        elif kind == "x":
-            p = int(token[1])
-            if p < 4:
-                flight["X"].append(same(bpiece(z + p, x - 1), xr))
-            if p > 0:
-                flight["X"].append(same(bpiece(z - p, x + 1), xl))
-            if p == 4:
-                mates += [same(bcolumn(x - 1), mate), same(bcolumn(x + 1), mate)]
+        elif token == "x0":
+            flight["X"].append(same(bcolumn(x - 1, 0, NZ // 2), xr))
+        elif token == "x1":
+            flight["X"].append(same(bcolumn(x + 1, NZ // 2, NZ // 2), xl))
+            mates += [same(bcolumn(x - 1), mate), same(bcolumn(x + 1), mate)]
         else:
             mates.append(same(bcolumn(x + 2), mate))
+            sent = len(copies) - 3
+            for c in copies[:sent]:
+                c.wait_send()
     get_grad.wait()
     arrived(mates)
-
-    def project(c):
-        def block(n, _):
-            cols = pl.ds(pl.multiple_of(n * 256, 256), 256)
-            w = wt[:, :, :, :, cols].reshape(NZ * NG * 64, 256)
-            dy = jnp.dot(gg[pl.ds(c * half, half), :], w, preferred_element_type=jnp.float32)
-            for r in range(c * half, (c + 1) * half, CH):
-                live = lax.broadcasted_iota(jnp.int32, (CH, LANES), 0) + r < count
-                for e in range(2):
-                    part = dy[r - c * half : r - c * half + CH, e * LANES : (e + 1) * LANES]
-                    part = part.astype(jnp.bfloat16).astype(jnp.float32)
-                    for s in range(3):
-                        dc = jnp.where(live, part * prod[s, 2 * n + e, r : r + CH, :], 0.0)
-                        dc32[s, 2 * n + e, r : r + CH, :] = dc.astype(jnp.bfloat16).astype(jnp.float32)
-            return 0
-
-        lax.fori_loop(0, groups // 2, block, 0)
-
-    def correlate(c):
-        def group(cg, _):
-            for s in range(3):
-                acc = [jnp.zeros((8, LANES), jnp.float32)] * taps
-                for r in range(c * half, (c + 1) * half, CH):
-                    dc = dc32[s, cg, r : r + CH, :]
-                    for j in range(taps):
-                        term = dc * u32[s, cg, 8 + r - j : 8 + r - j + CH, :]
-                        acc[j] = acc[j] + term.reshape(CH // 8, 8, LANES).sum(0)
-                if c == 0:
-                    fsc[cg, s] = jnp.zeros((8, LANES), jnp.float32)
-                for j in range(taps):
-                    term = acc[j].sum(0, keepdims=True)
-                    if c == 1:
-                        term = term + fsc[cg, s, j : j + 1, :]
-                    fsc[cg, s, j : j + 1, :] = term
-            return 0
-
-        lax.fori_loop(0, groups, group, 0)
-
     arrived(flight["g04"])
-    project(0)
-    head[...] = dc32[:, :, 0:8, :]
+    arrived(flight["g14"])
+
+    blocks = groups // 2
+
+    def both(b, _):
+        gate(jnp.maximum(b - 1, 0), (b + 1) % 2)
+        project(jnp.minimum(b, blocks - 1), b % 2)
+        return 0
+
+    lax.fori_loop(0, blocks + 1, both, 0)
     heads = push(head, heads_in, down, y)
-    correlate(0)
-    arrived(flight["g14"])
-    project(1)
-    correlate(1)
     f1 = []
     for d in range(1, NG):
         to = (q + d) % NG
@@ -277,27 +286,15 @@
     heads.wait_recv()
 
     def backward(cg, _):
-        lanes = pl.ds(pl.multiple_of(cg * LANES, LANES), LANES)
         for s in range(3):
-            zbuf[s, cg, 8:16, :] = jnp.where(i < n_ctx - 1, heads_in[s, cg], 0.0)
-
-        def insert(r, _):
-            r0 = pl.multiple_of(r * 8, 8)
-            at_row = jnp.clip(r0 - count, -8, 8) + 8
+            zbuf[s, cg, CH : CH + 8, :] = jnp.where(i < n_ctx - 1, heads_in[s, cg], 0.0)
+
+        for r in range(half, rows + 8, CH):
+            size = min(CH, rows + 8 - r)
+            row = jnp.clip(r - count, -CH, 8) + CH
             for s in range(3):
-                dc32[s, cg, pl.ds(r0, 8), :] += zbuf[s, cg, pl.ds(at_row, 8), :]
-            return 0
-
-        lax.fori_loop(rows // 16, rows // 8 + 1, insert, 0)
-        coef = [[filters_ref[s, pl.ds(j, 1), lanes] for j in range(taps)] for s in range(3)]
-
-        for r in range(0, rows, CH):
-            live = lax.broadcasted_iota(jnp.int32, (CH, LANES), 0) + r < count
-            for s in range(3):
-                acc = coef[s][0] * dc32[s, cg, r : r + CH, :]
-                for j in range(1, taps):
-                    acc = acc + coef[s][j] * dc32[s, cg, r + j : r + j + CH, :]
-                du32[s, cg, TILE + r : TILE + r + CH, :] = jnp.where(live, acc, 0.0)
+                dc32[s, cg, r : r + size, :] += zbuf[s, cg, pl.ds(row, size), :]
+        rows_back(cg, 0, rows)
 
         for s in range(3):
             for k in range(SLOTS):
@@ -343,7 +340,7 @@
         scales_ref[k] = jnp.where(last_slot >= k, scale, 0.0)
 
     arrived(f3)
-    for c in copies:
+    for c in copies[sent:]:
         c.wait_send()
 
 
@@ -378,8 +375,8 @@
     width = grad_out.shape[1]
     g = channels // LANES
     vmem = pl.BlockSpec(memory_space=pltpu.VMEM)
-    anywhere = pl.BlockSpec(memory_space=pl.ANY)
     smem = pl.BlockSpec(memory_space=pltpu.SMEM)
+    hbm = pl.BlockSpec(memory_space=pltpu.HBM)
     f32, bf16 = jnp.float32, jnp.bfloat16
     V = pltpu.VMEM
     du, inv, scale, fgrad = pl.pallas_call(
@@ -390,20 +387,22 @@
             V((SLOTS, 3 * g, LANES), f32),
             V((NG, 3, 8, LANES), f32),
         ),
-        in_specs=[anywhere, vmem, vmem, anywhere, smem, smem],
+        in_specs=[hbm, hbm, hbm, hbm, smem, smem],
         out_specs=(vmem, vmem, vmem, vmem),
         scratch_shapes=[
             V((3, rows, channels), bf16),
+            V((3, taps, channels), f32),
             V((3, g, rows + 8, LANES), f32),
             V((3, g, rows, LANES), f32),
             V((NZ, NX, NC, 64, channels), bf16),
             V((rows, NY * width), bf16),
+            V((2, rows, 256), f32),
             V((3, g, rows + 8, LANES), f32),
             V((3, g, 8, LANES), f32),
             V((3, g, 8, LANES), f32),
             V((3, g, 8, LANES), f32),
             V((3, g, 8, LANES), f32),
-            V((3, g, 24, LANES), f32),
+            V((3, g, 2 * CH + 8, LANES), f32),
             V((SLOTS, 3 * g, LANES), f32),
             V((3 * g, LANES), f32),
             V((3 * g, LANES), f32),
@@ -411,9 +410,9 @@
             V((g, 3, 8, LANES), f32),
             V((NG, 3, 8, LANES), f32),
             V((NZ, 3, 8, LANES), f32),
-            pltpu.SemaphoreType.DMA((128,)),
-            pltpu.SemaphoreType.DMA((128,)),
-            pltpu.SemaphoreType.DMA((2,)),
+            pltpu.SemaphoreType.DMA((96,)),
+            pltpu.SemaphoreType.DMA((96,)),
+            pltpu.SemaphoreType.DMA((4,)),
         ],
         compiler_params=pltpu.CompilerParams(
             collective_id=0, has_side_effects=True, vmem_limit_bytes=VLIM * 1024 * 1024

time: 79.1 us -> 81.3 us (1.028)
  Pallas kernels: 74.1 us -> 78.3 us
  local copies, waits for them, and re-layouts: 2.78 us -> 0 us
    pallas_call x1, Pallas kernels: 71.3 us -> 75.5 us  [shards(): pl.pallas_call(kernel, out_shape=(V((3, g, rows + 2 * TILE, LANES), f32),...]
    unnamed x6 -> x0, local copies, waits for them, and re-layouts: 2.78 us -> none
where the time goes in v4:
time: 81.3 us; the launch traced here: 80.3 us
  Pallas kernels  78.3 us (96%)
  between operations  1.93 us (2%)
    pallas_call x1, Pallas kernels, shards(): pl.pallas_call(kernel, out_shape=(V((3, g, rows + 2 * TILE, LANES), f32),...  75.5 us
    pallas_call x1, Pallas kernels, shards(): pl.pallas_call(finish, grid=(3,), out_shape=(jax.ShapeDtypeStruct((3, row...  2.86 us

profile of v4, /device:TPU:1, one launch (start us, length us, event | category | flops | bytes accessed | tf_op | source)
XLA Modules:
  0.0 80.3 jit_solution(4002642950463589851)
XLA Ops:
  1.9 75.5 %shard_map.85 = (f32[3,8,640,128]{3,2,1,0:T(8,128)S(1)}, f32[4,24,128]{2,1,0:T(8,128)S(1)}, f32[4,24,128]{2,1,0:T(8,128)S(1)}, f32[8,3,8,128]{3,2,1,0:T(8,128)S(1)}) custom-call(bf16[3,384,1024]{2,1,0:T(8,128)(2,1)} %streams_ref.1, f32[3,7,1024]{2,1,0:T(8,128)} %filters_ref.1, bf16[64,1024]{1,0:T(8,128)(2,1)} %bitcast.1, bf16[384,512]{1,0:T(8,128)(2,1)} %grad_ref.1, ...), custom_call_target="tpu_custom_call" | custom-call | flops 3221225472 | bytes 4718592 | tf_op jit(solution)/shard_map/pallas_call | solution.py:382
  77.4 2.9 %shard_map.86 = (bf16[3,384,1024]{2,1,0:T(8,128)(2,1)}, f32[3,4,1024]{2,1,0:T(4,128)}, f32[3,7,1024]{2,1,0:T(8,128)}) custom-call(s32[1]{0:T(128)S(6)} %copy.10.starts_ref, f32[3,8,640,128]{3,2,1,0:T(8,128)S(1)} %get-tuple-element.7.du_ref, f32[4,24,128]{2,1,0:T(8,128)S(1)} %get-tuple-element.8.inv_ref, f32[4,24,128]{2,1,0:T(8,128)S(1)} %get-tuple-element.9.scale_ref, ...), custom_call_target="tpu_custom_call" | custom-call | tf_op jit(solution)/shard_map/pallas_call | solution.py:424

commit v5 on v4

--- a/solution.py
+++ b/solution.py
@@ -18,7 +18,7 @@
 
 
 ORDER = (
-    "b1", "b2", "g01", "a0", "b3", "b4", "f", "g11", "f", "f", "A01", "f", "g02", "A11", "x0",
+    "b1", "m", "b2", "a0", "g01", "b3", "b4", "f", "f", "g11", "f", "f", "A01", "g02", "A11", "x0",
     "A02", "g12", "A12", "x1", "g03", "A03", "A13", "g13", "X", "A04", "A14",
 )
 
@@ -26,9 +26,9 @@
 def kernel(
     streams_ref, filters_ref, weight_ref, grad_ref, counts_ref, starts_ref,
     du32, inv_ref, scales_ref, fgrad_ref,
-    sv, fv, u32, prod, wt, gg, dyb, dc32, tail, halo, head, heads_in, zbuf,
+    sv, fv, gv, give, u32, prod, wt, gg, own_dy, part_out, part_in, dc32, tail, halo, head, heads_in, zbuf,
     msc, tmx, max_prev, max_next, fsc, p1, p2,
-    send, recv, local,
+    send, recv, psend, precv, local,
 ):
     rows = grad_ref.shape[0]
     width = grad_ref.shape[1]
@@ -70,11 +70,10 @@
 
     get_streams = pltpu.make_async_copy(streams_ref, sv, local.at[0])
     get_streams.start()
-    own_cols = pl.ds(pl.multiple_of(y * width, width), width)
-    get_grad = pltpu.make_async_copy(grad_ref, gg.at[:, own_cols], local.at[1])
+    get_grad = pltpu.make_async_copy(grad_ref, gv, local.at[1])
     get_grad.start()
 
-    get_weight = pltpu.make_async_copy(weight_ref, wt.at[z, x, core], local.at[2])
+    get_weight = pltpu.make_async_copy(weight_ref, wt.at[z, x], local.at[2])
     get_weight.start()
     get_filters = pltpu.make_async_copy(filters_ref, fv, local.at[3])
     get_filters.start()
@@ -85,23 +84,37 @@
     peers += [(((z + d) % NZ) * NG + q, y) for d in range(1, NZ)]
     for peer in peers:
         pl.semaphore_signal(barrier, inc=1, device_id=peer, device_id_type=MESH)
+
+    half = rows // 2
+    keep = width // 2
+    mine = pl.ds(pl.multiple_of(y * keep, keep), keep)
+    get_grad.wait()
+
+    def sort_columns(r, _):
+        r0 = pl.multiple_of(r * CH, CH)
+        v = gv[pl.ds(r0, CH), :].astype(jnp.float32)
+        piece = [v[:, 64 * e : 64 * (e + 1)] for e in range(NG)]
+        even = jnp.concatenate(piece[0::2], axis=1)
+        odd = jnp.concatenate(piece[1::2], axis=1)
+        gg[pl.ds(r0, CH), mine] = jnp.where(core == 0, even, odd).astype(jnp.bfloat16)
+        give[pl.ds(r0, CH), :] = jnp.where(core == 0, odd, even).astype(jnp.bfloat16)
+        return 0
+
+    lax.fori_loop(0, rows // CH, sort_columns, 0)
     pl.semaphore_wait(barrier, len(peers))
-
-    half = rows // 2
 
     def gblock(c, t):
         t = (t + NY) % NY
-        return gg.at[pl.ds(c * half, half), pl.ds(pl.multiple_of(t * width, width), width)]
+        return gg.at[pl.ds(c * rows, rows), pl.ds(pl.multiple_of(t * keep, keep), keep)]
 
     def gstep(c, d):
         out = []
-        own = grad_ref.at[pl.ds(c * half, half)]
         if d < 4 or c == 0:
             block = gblock(c, y - d + 1)
-            out.append(push(own if d == 1 else block, block, i, yr))
+            out.append(push(block, block, i, yr))
         if d < 4 or c == 1:
             block = gblock(c, y + d - 1)
-            out.append(push(own if d == 1 else block, block, i, yl))
+            out.append(push(block, block, i, yl))
         return out
 
     def arrived(cs):
@@ -109,13 +122,13 @@
             c.wait_recv()
 
     def ablock(c, zz, many=2):
-        return wt.at[(zz + NZ) % NZ, pl.ds(2 * c, many), core, pl.ds(0, 32), :]
+        return wt.at[(zz + NZ) % NZ, pl.ds(2 * c, many), pl.ds(0, 32), :]
 
     def bpiece(zz, lo=32, many=32):
-        return wt.at[(zz + NZ) % NZ, x, core, pl.ds(lo, many), :]
+        return wt.at[(zz + NZ) % NZ, x, pl.ds(lo, many), :]
 
     def bcolumn(xx, lo=0, many=NZ):
-        return wt.at[pl.ds(lo, many), (xx + NX) % NX, core, pl.ds(32, 32), :]
+        return wt.at[pl.ds(lo, many), (xx + NX) % NX, pl.ds(32, 32), :]
 
     def same(block, dest):
         return push(block, block, dest, y)
@@ -137,13 +150,12 @@
         return [same(block, xr), same(block, xl)]
 
     flight = {"X": []}
-    mates = []
+    flight["m"] = [push(give, gg.at[pl.ds(rows, rows), mine], mate, y)]
     flight["g01"] = gstep(0, 1)
     get_weight.wait()
     flight["b1"] = bstep(1)
-    own = wt.at[z, x, core, pl.ds(0, 32), :]
+    own = wt.at[z, x, pl.ds(0, 32), :]
     flight["a0"] = [same(own, at(z, x + d, core)) for d in range(1, NX)]
-    flight["g11"] = gstep(1, 1)
 
     get_streams.wait()
 
@@ -187,16 +199,25 @@
         return 0
 
     def project(b, slot):
-        cols = pl.ds(pl.multiple_of(b * 256, 256), 256)
-        w = wt[:, :, :, :, cols].reshape(NZ * NG * 64, 256)
-        dy = jnp.dot(gg[...], w, preferred_element_type=jnp.float32)
-        dyb[slot] = dy.astype(jnp.bfloat16).astype(jnp.float32)
-
-    def gate(b, slot):
+        cols = pl.ds(pl.multiple_of(jnp.minimum(b, blocks - 1) * 256, 256), 256)
+        w = wt[:, :, :, cols].reshape(NZ * NX * 64, 256)
+        theirs = jnp.dot(gg[rows:, :], w, preferred_element_type=jnp.float32)
+        part_out[b] = theirs.astype(jnp.bfloat16)
+        own_dy[slot] = jnp.dot(gg[:rows, :], w, preferred_element_type=jnp.float32)
+
+    def partial(b):
+        return pltpu.make_async_remote_copy(
+            src_ref=part_out.at[b], dst_ref=part_in.at[b], send_sem=psend.at[b], recv_sem=precv.at[b],
+            device_id=(mate, y), device_id_type=MESH,
+        )
+
+    def gate(b, slot, got):
         for r in range(0, rows, CH):
             live = lax.broadcasted_iota(jnp.int32, (CH, LANES), 0) + r < count
             for e in range(2):
-                dy = dyb[slot, r : r + CH, e * LANES : (e + 1) * LANES]
+                lanes = slice(e * LANES, (e + 1) * LANES)
+                dy = own_dy[slot, r : r + CH, lanes] + part_in[got, r : r + CH, lanes].astype(jnp.float32)
+                dy = dy.astype(jnp.bfloat16).astype(jnp.float32)
                 for s in range(3):
                     dc = jnp.where(live, dy * prod[s, 2 * b + e, r : r + CH, :], 0.0)
                     dc32[s, 2 * b + e, r : r + CH, :] = dc.astype(jnp.bfloat16).astype(jnp.float32)
@@ -224,6 +245,7 @@
                     acc = acc + coef[s][j] * dc32[s, cg, r + j : r + j + CH, :]
                 du32[s, cg, TILE + r : TILE + r + CH, :] = jnp.where(live, acc, 0.0)
 
+    blocks = groups // 2
     done = 0
     for token in ORDER:
         kind = token[0]
@@ -239,12 +261,8 @@
             c, d = int(token[1]), int(token[2])
             if d < 4:
                 flight[f"{kind}{c}{d + 1}"] = (gstep if kind == "g" else astep)(c, d + 1)
-            if kind == "A" and c == 1:
-                mates.append(same(ablock(0, z - d, NX), mate))
-                if d < 4:
-                    mates.append(same(ablock(0, z + d, NX), mate))
-        elif kind == "a":
-            mates.append(same(ablock(0, z, NX), mate))
+        elif kind == "m":
+            flight["g11"] = gstep(1, 1)
         elif kind == "b":
             d = int(token[1])
             if d < 4:
@@ -253,27 +271,29 @@
                 flight["A01"], flight["A11"] = astep(0, 1), astep(1, 1)
             if d == 4:
                 flight["x0"], flight["x1"] = xstep(0), xstep(1)
-                mates.append(same(bcolumn(x), mate))
         elif token == "x0":
             flight["X"].append(same(bcolumn(x - 1, 0, NZ // 2), xr))
         elif token == "x1":
             flight["X"].append(same(bcolumn(x + 1, NZ // 2, NZ // 2), xl))
-            mates += [same(bcolumn(x - 1), mate), same(bcolumn(x + 1), mate)]
-        else:
-            mates.append(same(bcolumn(x + 2), mate))
-            sent = len(copies) - 3
+        elif token == "X":
+            sent = len(copies) - 2
             for c in copies[:sent]:
                 c.wait_send()
-    get_grad.wait()
-    arrived(mates)
     arrived(flight["g04"])
     arrived(flight["g14"])
 
-    blocks = groups // 2
-
     def both(b, _):
-        gate(jnp.maximum(b - 1, 0), (b + 1) % 2)
-        project(jnp.minimum(b, blocks - 1), b % 2)
+        @pl.when(b >= 1)
+        def _():
+            partial(b - 1).wait_recv()
+
+        gate(jnp.maximum(b - 1, 0), (b + 1) % 2, (b + blocks) % (blocks + 1))
+        project(b, b % 2)
+
+        @pl.when(b < blocks)
+        def _():
+            partial(b).start()
+
         return 0
 
     lax.fori_loop(0, blocks + 1, both, 0)
@@ -342,6 +362,8 @@
     arrived(f3)
     for c in copies[sent:]:
         c.wait_send()
+    for b in range(blocks):
+        partial(b).wait_send()
 
 
 def finish(starts_ref, du_ref, inv_ref, scale_ref, fgrad_ref, pay_out, scales_out, fgrad_out):
@@ -392,11 +414,15 @@
         scratch_shapes=[
             V((3, rows, channels), bf16),
             V((3, taps, channels), f32),
+            V((rows, width), bf16),
+            V((rows, width // 2), bf16),
             V((3, g, rows + 8, LANES), f32),
             V((3, g, rows, LANES), f32),
-            V((NZ, NX, NC, 64, channels), bf16),
-            V((rows, NY * width), bf16),
+            V((NZ, NX, 64, channels), bf16),
+            V((2 * rows, NY * width // 2), bf16),
             V((2, rows, 256), f32),
+            V((g // 2 + 1, rows, 256), bf16),
+            V((g // 2 + 1, rows, 256), bf16),
             V((3, g, rows + 8, LANES), f32),
             V((3, g, 8, LANES), f32),
             V((3, g, 8, LANES), f32),
@@ -412,6 +438,8 @@
             V((NZ, 3, 8, LANES), f32),
             pltpu.SemaphoreType.DMA((96,)),
             pltpu.SemaphoreType.DMA((96,)),
+            pltpu.SemaphoreType.DMA((g // 2,)),
+            pltpu.SemaphoreType.DMA((g // 2,)),
             pltpu.SemaphoreType.DMA((4,)),
         ],
         compiler_params=pltpu.CompilerParams(

time: 81.3 us -> 85.6 us (1.053)
  Pallas kernels: 78.3 us -> 83.3 us
    pallas_call x1, Pallas kernels: 75.5 us -> 80.5 us  [shards(): pl.pallas_call(kernel, out_shape=(V((3, g, rows + 2 * TILE, LANES), f32),...]
where the time goes in v5:
time: 85.6 us; the launch traced here: 85.3 us
  Pallas kernels  83.3 us (97%)
  between operations  1.93 us (2%)
    pallas_call x1, Pallas kernels, shards(): pl.pallas_call(kernel, out_shape=(V((3, g, rows + 2 * TILE, LANES), f32),...  80.5 us
    pallas_call x1, Pallas kernels, shards(): pl.pallas_call(finish, grid=(3,), out_shape=(jax.ShapeDtypeStruct((3, row...  2.86 us

profile of v5, /device:TPU:1, one launch (start us, length us, event | category | flops | bytes accessed | tf_op | source)
XLA Modules:
  0.0 85.3 jit_solution(5567495537490439797)
XLA Ops:
  1.9 80.5 %shard_map.85 = (f32[3,8,640,128]{3,2,1,0:T(8,128)S(1)}, f32[4,24,128]{2,1,0:T(8,128)S(1)}, f32[4,24,128]{2,1,0:T(8,128)S(1)}, f32[8,3,8,128]{3,2,1,0:T(8,128)S(1)}) custom-call(bf16[3,384,1024]{2,1,0:T(8,128)(2,1)} %streams_ref.1, f32[3,7,1024]{2,1,0:T(8,128)} %filters_ref.1, bf16[64,1024]{1,0:T(8,128)(2,1)} %bitcast.1, bf16[384,512]{1,0:T(8,128)(2,1)} %grad_ref.1, ...), custom_call_target="tpu_custom_call" | custom-call | flops 3221225472 | bytes 4718592 | tf_op jit(solution)/shard_map/pallas_call | solution.py:404
  82.4 2.9 %shard_map.86 = (bf16[3,384,1024]{2,1,0:T(8,128)(2,1)}, f32[3,4,1024]{2,1,0:T(4,128)}, f32[3,7,1024]{2,1,0:T(8,128)}) custom-call(s32[1]{0:T(128)S(6)} %copy.10.starts_ref, f32[3,8,640,128]{3,2,1,0:T(8,128)S(1)} %get-tuple-element.7.du_ref, f32[4,24,128]{2,1,0:T(8,128)S(1)} %get-tuple-element.8.inv_ref, f32[4,24,128]{2,1,0:T(8,128)S(1)} %get-tuple-element.9.scale_ref, ...), custom_call_target="tpu_custom_call" | custom-call | tf_op jit(solution)/shard_map/pallas_call | solution.py:452

commit v6 on v4

--- a/solution.py
+++ b/solution.py
@@ -14,6 +14,7 @@
 NG = NX * NC
 CH = 64
 SLOTS = 4
+STEP = 49
 VLIM = 54
 
 
@@ -151,78 +152,70 @@
         lanes = pl.ds(pl.multiple_of(cg * LANES, LANES), LANES)
         for s in range(3):
             u32[s, cg, 8 : 8 + rows, :] = sv[s, :, lanes].astype(jnp.float32)
+            u32[s, cg, 8 + rows :, :] = jnp.zeros((8, LANES), jnp.float32)
             tail[s, cg] = u32[s, cg, pl.ds(jnp.clip(count, 8, rows), 8), :]
         return 0
 
     lax.fori_loop(0, groups, widen, 0)
     tails = push(tail, halo, up, y)
+
+    def strided(start):
+        return pl.ds(start, 8, stride=STEP)
+
+    def tapped(f, w):
+        acc = f[0] * w[0]
+        for j in range(1, taps):
+            acc = acc + f[j] * w[j]
+        return acc
+
+    sub = lax.broadcasted_iota(jnp.int32, (8, LANES), 0) * STEP
 
     def forward(cg, _):
         lanes = pl.ds(pl.multiple_of(cg * LANES, LANES), LANES)
         coef = []
         for s in range(3):
             u32[s, cg, 0:8, :] = jnp.where(i > 0, halo[s, cg], 0.0)
-            du32[s, cg, 0:TILE, :] = jnp.zeros((TILE, LANES), jnp.float32)
-            du32[s, cg, TILE + rows :, :] = jnp.zeros((TILE, LANES), jnp.float32)
-            dc32[s, cg, rows:, :] = jnp.zeros((8, LANES), jnp.float32)
-            zbuf[s, cg] = jnp.zeros((2 * CH + 8, LANES), jnp.float32)
+            dc32[s, cg, rows:, :] = jnp.zeros((16, LANES), jnp.float32)
+            zbuf[s, cg] = jnp.zeros((rows + 16, LANES), jnp.float32)
             for k in range(taps, 8):
                 fsc[cg, s, k : k + 1, :] = jnp.zeros((1, LANES), jnp.float32)
             coef.append([fv[s, pl.ds(j, 1), lanes] for j in range(taps)])
 
-        def chunk(r, _):
-            r0 = pl.multiple_of(r * CH, CH)
+        spread = [[jnp.broadcast_to(f, (8, LANES)) for f in fs] for fs in coef]
+        window = [[u32[s, cg, strided(8 - j), :] for j in range(1, taps)] for s in range(3)]
+        for k in range(STEP):
             c = []
             for s in range(3):
-                acc = coef[s][0] * u32[s, cg, pl.ds(8 + r0, CH), :]
-                for j in range(1, taps):
-                    acc = acc + coef[s][j] * u32[s, cg, pl.ds(8 + r0 - j, CH), :]
-                c.append(acc)
-            prod[0, cg, pl.ds(r0, CH), :] = c[1] * c[2]
-            prod[1, cg, pl.ds(r0, CH), :] = c[0] * c[2]
-            prod[2, cg, pl.ds(r0, CH), :] = c[0] * c[1]
-            return 0
-
-        lax.fori_loop(0, rows // CH, chunk, 0)
+                window[s] = [u32[s, cg, strided(8 + k), :]] + window[s][: taps - 1]
+                c.append(tapped(spread[s], window[s]))
+            prod[0, cg, k] = c[1] * c[2]
+            prod[1, cg, k] = c[0] * c[2]
+            prod[2, cg, k] = c[0] * c[1]
         return 0
 
     def project(b, slot):
         cols = pl.ds(pl.multiple_of(b * 256, 256), 256)
         w = wt[:, :, :, :, cols].reshape(NZ * NG * 64, 256)
         dy = jnp.dot(gg[...], w, preferred_element_type=jnp.float32)
-        dyb[slot] = dy.astype(jnp.bfloat16).astype(jnp.float32)
+        dy = dy.astype(jnp.bfloat16).astype(jnp.float32)
+        dyb[slot, 0, :rows, :] = dy[:, :LANES]
+        dyb[slot, 1, :rows, :] = dy[:, LANES:]
 
     def gate(b, slot):
-        for r in range(0, rows, CH):
-            live = lax.broadcasted_iota(jnp.int32, (CH, LANES), 0) + r < count
-            for e in range(2):
-                dy = dyb[slot, r : r + CH, e * LANES : (e + 1) * LANES]
-                for s in range(3):
-                    dc = jnp.where(live, dy * prod[s, 2 * b + e, r : r + CH, :], 0.0)
-                    dc32[s, 2 * b + e, r : r + CH, :] = dc.astype(jnp.bfloat16).astype(jnp.float32)
         for e in range(2):
             cg = 2 * b + e
             for s in range(3):
                 acc = [jnp.zeros((8, LANES), jnp.float32)] * taps
-                head[s, cg] = dc32[s, cg, 0:8, :]
-                for r in range(0, rows, CH):
-                    dc = dc32[s, cg, r : r + CH, :]
-                    for j in range(taps):
-                        term = dc * u32[s, cg, 8 + r - j : 8 + r - j + CH, :]
-                        acc[j] = acc[j] + term.reshape(CH // 8, 8, LANES).sum(0)
+                window = [u32[s, cg, strided(8 - j), :] for j in range(1, taps)]
+                for k in range(STEP):
+                    window = [u32[s, cg, strided(8 + k), :]] + window[: taps - 1]
+                    dc = jnp.where(sub < count - k, dyb[slot, e, strided(k), :] * prod[s, cg, k], 0.0)
+                    dc = dc.astype(jnp.bfloat16).astype(jnp.float32)
+                    dc32[s, cg, strided(k), :] = dc
+                    acc = [acc[j] + dc * window[j] for j in range(taps)]
                 for j in range(taps):
                     fsc[cg, s, j : j + 1, :] = acc[j].sum(0, keepdims=True)
-
-    def rows_back(cg, lo, hi):
-        lanes = pl.ds(pl.multiple_of(cg * LANES, LANES), LANES)
-        coef = [[fv[s, pl.ds(j, 1), lanes] for j in range(taps)] for s in range(3)]
-        for r in range(lo, hi, CH):
-            live = lax.broadcasted_iota(jnp.int32, (CH, LANES), 0) + r < count
-            for s in range(3):
-                acc = coef[s][0] * dc32[s, cg, r : r + CH, :]
-                for j in range(1, taps):
-                    acc = acc + coef[s][j] * dc32[s, cg, r + j : r + j + CH, :]
-                du32[s, cg, TILE + r : TILE + r + CH, :] = jnp.where(live, acc, 0.0)
+                head[s, cg] = dc32[s, cg, 0:8, :]
 
     done = 0
     for token in ORDER:
@@ -285,22 +278,36 @@
 
     heads.wait_recv()
 
+    held = jnp.clip(count, half, rows)
+
     def backward(cg, _):
+        lanes = pl.ds(pl.multiple_of(cg * LANES, LANES), LANES)
         for s in range(3):
-            zbuf[s, cg, CH : CH + 8, :] = jnp.where(i < n_ctx - 1, heads_in[s, cg], 0.0)
-
-        for r in range(half, rows + 8, CH):
-            size = min(CH, rows + 8 - r)
-            row = jnp.clip(r - count, -CH, 8) + CH
+            zbuf[s, cg, half : half + 8, :] = jnp.where(i < n_ctx - 1, heads_in[s, cg], 0.0)
+
+        leap = (rows - half + 8) // 8
+        for m in range(leap):
+            to = pl.ds(half + m, 8, stride=leap)
             for s in range(3):
-                dc32[s, cg, r : r + size, :] += zbuf[s, cg, pl.ds(row, size), :]
-        rows_back(cg, 0, rows)
-
+                dc32[s, cg, to, :] += zbuf[s, cg, pl.ds(rows + m - held, 8, stride=leap), :]
+
+        low = (sub + offset) // TILE
+        border = (low + 1) * TILE - offset - sub
         for s in range(3):
+            f = [jnp.broadcast_to(fv[s, pl.ds(j, 1), lanes], (8, LANES)) for j in range(taps)]
+            window = [dc32[s, cg, strided(j), :] for j in range(taps - 1)]
+            before = jnp.zeros((8, LANES), jnp.float32)
+            after = before
+            for k in range(STEP):
+                window = window[-(taps - 1) :] + [dc32[s, cg, strided(k + taps - 1), :]]
+                du = jnp.where(sub < count - k, tapped(f, window), 0.0)
+                du32[s, cg, strided(k), :] = du
+                size = jnp.abs(du)
+                before = jnp.maximum(before, jnp.where(border > k, size, 0.0))
+                after = jnp.maximum(after, jnp.where(border > k, 0.0, size))
             for k in range(SLOTS):
-                block = jnp.abs(du32[s, cg, pl.ds((k + 1) * TILE - offset, TILE), :])
-                top = block.reshape(TILE // 8, 8, LANES).max(0).max(0, keepdims=True)
-                msc[k, pl.ds(s * groups + cg, 1), :] = top
+                top = jnp.maximum(jnp.where(low == k, before, 0.0), jnp.where(low == k - 1, after, 0.0))
+                msc[k, pl.ds(s * groups + cg, 1), :] = top.max(0, keepdims=True)
         return 0
 
     lax.fori_loop(0, groups // 2, backward, 0)
@@ -362,7 +369,7 @@
             scale = jnp.where(pos >= 3 * TILE, inv[3], inv[2])
             scale = jnp.where(pos >= 2 * TILE, scale, inv[1])
             scale = jnp.where(pos >= TILE, scale, inv[0])
-            du = du_ref[s, cg, TILE + r : TILE + r + CH, :]
+            du = du_ref[s, cg, r : r + CH, :]
             pay_out[0, r : r + CH, lanes] = (du * scale).astype(jnp.bfloat16)
         return 0
 
@@ -382,7 +389,7 @@
     du, inv, scale, fgrad = pl.pallas_call(
         kernel,
         out_shape=(
-            V((3, g, rows + 2 * TILE, LANES), f32),
+            V((3, g, rows + 8, LANES), f32),
             V((SLOTS, 3 * g, LANES), f32),
             V((SLOTS, 3 * g, LANES), f32),
             V((NG, 3, 8, LANES), f32),
@@ -392,17 +399,17 @@
         scratch_shapes=[
             V((3, rows, channels), bf16),
             V((3, taps, channels), f32),
-            V((3, g, rows + 8, LANES), f32),
-            V((3, g, rows, LANES), f32),
+            V((3, g, rows + 16, LANES), f32),
+            V((3, g, STEP, 8, LANES), f32),
             V((NZ, NX, NC, 64, channels), bf16),
             V((rows, NY * width), bf16),
-            V((2, rows, 256), f32),
-            V((3, g, rows + 8, LANES), f32),
+            V((2, 2, rows + 8, LANES), f32),
+            V((3, g, rows + 16, LANES), f32),
             V((3, g, 8, LANES), f32),
             V((3, g, 8, LANES), f32),
             V((3, g, 8, LANES), f32),
             V((3, g, 8, LANES), f32),
-            V((3, g, 2 * CH + 8, LANES), f32),
+            V((3, g, rows + 16, LANES), f32),
             V((SLOTS, 3 * g, LANES), f32),
             V((3 * g, LANES), f32),
             V((3 * g, LANES), f32),

time: 81.3 us -> 80.7 us (level)
  no operation moved by 1% of the time
where the time goes in v6:
time: 80.7 us; the launch traced here: 79.8 us
  Pallas kernels  77.9 us (97%)
  between operations  1.93 us (2%)
    pallas_call x1, Pallas kernels, shards(): pl.pallas_call(kernel, out_shape=(V((3, g, rows + 8, LANES), f32), V((SLO...  75 us
    pallas_call x1, Pallas kernels, shards(): pl.pallas_call(finish, grid=(3,), out_shape=(jax.ShapeDtypeStruct((3, row...  2.86 us

profile of v6, /device:TPU:1, one launch (start us, length us, event | category | flops | bytes accessed | tf_op | source)
XLA Modules:
  0.0 79.8 jit_solution(13558855037728515497)
XLA Ops:
  1.9 75.0 %shard_map.85 = (f32[3,8,392,128]{3,2,1,0:T(8,128)S(1)}, f32[4,24,128]{2,1,0:T(8,128)S(1)}, f32[4,24,128]{2,1,0:T(8,128)S(1)}, f32[8,3,8,128]{3,2,1,0:T(8,128)S(1)}) custom-call(bf16[3,384,1024]{2,1,0:T(8,128)(2,1)} %streams_ref.1, f32[3,7,1024]{2,1,0:T(8,128)} %filters_ref.1, bf16[64,1024]{1,0:T(8,128)(2,1)} %bitcast.1, bf16[384,512]{1,0:T(8,128)(2,1)} %grad_ref.1, ...), custom_call_target="tpu_custom_call" | custom-call | flops 3221225472 | bytes 4718592 | tf_op jit(solution)/shard_map/pallas_call | solution.py:389
  77.0 2.9 %shard_map.86 = (bf16[3,384,1024]{2,1,0:T(8,128)(2,1)}, f32[3,4,1024]{2,1,0:T(4,128)}, f32[3,7,1024]{2,1,0:T(8,128)}) custom-call(s32[1]{0:T(128)S(6)} %copy.10.starts_ref, f32[3,8,392,128]{3,2,1,0:T(8,128)S(1)} %get-tuple-element.7.du_ref, f32[4,24,128]{2,1,0:T(8,128)S(1)} %get-tuple-element.8.inv_ref, f32[4,24,128]{2,1,0:T(8,128)S(1)} %get-tuple-element.9.scale_ref, ...), custom_call_target="tpu_custom_call" | custom-call | tf_op jit(solution)/shard_map/pallas_call | solution.py:431

commit v7 on v6

--- a/solution.py
+++ b/solution.py
@@ -19,8 +19,8 @@
 
 
 ORDER = (
-    "b1", "b2", "g01", "a0", "b3", "b4", "f", "g11", "f", "f", "A01", "f", "g02", "A11", "x0",
-    "A02", "g12", "A12", "x1", "g03", "A03", "A13", "g13", "X", "A04", "A14",
+    "b1", "f", "g01", "a0", "f", "b2", "x0", "f", "x1", "g11", "A01", "x2", "f", "A11", "g02",
+    "b3", "A02", "g12", "x3", "A12", "b4", "g03", "A03", "x4", "A13", "g13", "X", "A04", "A14",
 )
 
 
@@ -29,7 +29,7 @@
     du32, inv_ref, scales_ref, fgrad_ref,
     sv, fv, u32, prod, wt, gg, dyb, dc32, tail, halo, head, heads_in, zbuf,
     msc, tmx, max_prev, max_next, fsc, p1, p2,
-    send, recv, local,
+    send, recv, hsend, hrecv, tsend, trecv, local,
 ):
     rows = grad_ref.shape[0]
     width = grad_ref.shape[1]
@@ -112,11 +112,11 @@
     def ablock(c, zz, many=2):
         return wt.at[(zz + NZ) % NZ, pl.ds(2 * c, many), core, pl.ds(0, 32), :]
 
-    def bpiece(zz, lo=32, many=32):
-        return wt.at[(zz + NZ) % NZ, x, core, pl.ds(lo, many), :]
-
-    def bcolumn(xx, lo=0, many=NZ):
-        return wt.at[pl.ds(lo, many), (xx + NX) % NX, core, pl.ds(32, 32), :]
+    def bpiece(zz, xx, lo=32, many=32):
+        return wt.at[(zz + NZ) % NZ, (xx + NX) % NX, core, pl.ds(lo, many), :]
+
+    def bcolumn(xx):
+        return wt.at[:, (xx + NX) % NX, core, pl.ds(32, 32), :]
 
     def same(block, dest):
         return push(block, block, dest, y)
@@ -131,11 +131,13 @@
 
     def bstep(d):
         many = 32 if d < 4 else 16
-        return [same(bpiece(z - d + 1, 32, many), zr), same(bpiece(z + d - 1, 64 - many, many), zl)]
-
-    def xstep(h):
-        block = bcolumn(x, h * NZ // 2, NZ // 2)
-        return [same(block, xr), same(block, xl)]
+        return [same(bpiece(z - d + 1, x, 32, many), zr), same(bpiece(z + d - 1, x, 64 - many, many), zl)]
+
+    def xstep(p):
+        out = []
+        for zz in [z + p] if p in (0, 4) else [z + p, z - p]:
+            out += [same(bpiece(zz, x), xr), same(bpiece(zz, x), xl)]
+        return out
 
     flight = {"X": []}
     mates = []
@@ -144,6 +146,7 @@
     flight["b1"] = bstep(1)
     own = wt.at[z, x, core, pl.ds(0, 32), :]
     flight["a0"] = [same(own, at(z, x + d, core)) for d in range(1, NX)]
+    flight["x0"] = xstep(0)
     flight["g11"] = gstep(1, 1)
 
     get_streams.wait()
@@ -237,21 +240,23 @@
                 if d < 4:
                     mates.append(same(ablock(0, z + d, NX), mate))
         elif kind == "a":
+            flight["A01"], flight["A11"] = astep(0, 1), astep(1, 1)
             mates.append(same(ablock(0, z, NX), mate))
         elif kind == "b":
             d = int(token[1])
             if d < 4:
                 flight[f"b{d + 1}"] = bstep(d + 1)
-            if d == 3:
-                flight["A01"], flight["A11"] = astep(0, 1), astep(1, 1)
-            if d == 4:
-                flight["x0"], flight["x1"] = xstep(0), xstep(1)
+            else:
                 mates.append(same(bcolumn(x), mate))
-        elif token == "x0":
-            flight["X"].append(same(bcolumn(x - 1, 0, NZ // 2), xr))
-        elif token == "x1":
-            flight["X"].append(same(bcolumn(x + 1, NZ // 2, NZ // 2), xl))
-            mates += [same(bcolumn(x - 1), mate), same(bcolumn(x + 1), mate)]
+            flight[f"x{d}"] = xstep(d)
+        elif kind == "x":
+            p = int(token[1])
+            if p < 4:
+                flight["X"].append(same(bpiece(z + p, x - 1), xr))
+            if p > 0:
+                flight["X"].append(same(bpiece(z - p, x + 1), xl))
+            if p == 4:
+                mates += [same(bcolumn(x - 1), mate), same(bcolumn(x + 1), mate)]
         else:
             mates.append(same(bcolumn(x + 2), mate))
             sent = len(copies) - 3
@@ -264,23 +269,45 @@
 
     blocks = groups // 2
 
+    def head_copy(b):
+        two = pl.ds(2 * b, 2)
+        return pltpu.make_async_remote_copy(
+            src_ref=head.at[:, two], dst_ref=heads_in.at[:, two], send_sem=hsend.at[b], recv_sem=hrecv.at[b],
+            device_id=(down, y), device_id_type=MESH,
+        )
+
+    def term_copy(to, me):
+        return pltpu.make_async_remote_copy(
+            src_ref=fsc.at[to], dst_ref=p1.at[me], send_sem=tsend.at[to], recv_sem=trecv.at[me],
+            device_id=(z * NG + to, y), device_id_type=MESH,
+        )
+
+    def leave(b):
+        head_copy(b).start()
+        for e in range(2):
+            @pl.when(2 * b + e != q)
+            def _():
+                term_copy(2 * b + e, q).start()
+
     def both(b, _):
-        gate(jnp.maximum(b - 1, 0), (b + 1) % 2)
-        project(jnp.minimum(b, blocks - 1), b % 2)
-        return 0
-
-    lax.fori_loop(0, blocks + 1, both, 0)
-    heads = push(head, heads_in, down, y)
-    f1 = []
-    for d in range(1, NG):
-        to = (q + d) % NG
-        f1.append(push(fsc.at[to], p1.at[d], z * NG + to, y))
-
-    heads.wait_recv()
+        gate(b - 1, (b + 1) % 2)
+        project(b, b % 2)
+        leave(b - 1)
+        return 0
+
+    project(0, 0)
+    lax.fori_loop(1, blocks, both, 0)
+    gate(blocks - 1, (blocks - 1) % 2)
+    leave(blocks - 1)
 
     held = jnp.clip(count, half, rows)
 
-    def backward(cg, _):
+    def backward(b, _):
+        head_copy(b).wait_recv()
+        lax.fori_loop(2 * b, 2 * b + 2, group_back, 0)
+        return 0
+
+    def group_back(cg, _):
         lanes = pl.ds(pl.multiple_of(cg * LANES, LANES), LANES)
         for s in range(3):
             zbuf[s, cg, half : half + 8, :] = jnp.where(i < n_ctx - 1, heads_in[s, cg], 0.0)
@@ -310,16 +337,17 @@
                 msc[k, pl.ds(s * groups + cg, 1), :] = top.max(0, keepdims=True)
         return 0
 
-    lax.fori_loop(0, groups // 2, backward, 0)
-    arrived(f1)
+    lax.fori_loop(0, blocks // 2, backward, 0)
     part = fsc[q]
     for d in range(1, NG):
-        part = part + p1[d]
+        source = (q + d) % NG
+        term_copy(source, source).wait_recv()
+        part = part + p1[source]
     p2[z] = part
     f2 = []
     for d in range(1, NZ):
         f2.append(push(p2.at[z], p2.at[z], ((z + d) % NZ) * NG + q, y))
-    lax.fori_loop(groups // 2, groups, backward, 0)
+    lax.fori_loop(blocks // 2, blocks, backward, 0)
     tmx[...] = msc[last_slot]
     to_next = push(tmx, max_prev, up, y)
     to_prev = push(msc.at[0], max_next, down, y)
@@ -349,6 +377,10 @@
     arrived(f3)
     for c in copies[sent:]:
         c.wait_send()
+    for b in range(blocks):
+        head_copy(b).wait_send()
+    for d in range(1, NG):
+        term_copy((q + d) % NG, q).wait_send()
 
 
 def finish(starts_ref, du_ref, inv_ref, scale_ref, fgrad_ref, pay_out, scales_out, fgrad_out):
@@ -417,8 +449,12 @@
             V((g, 3, 8, LANES), f32),
             V((NG, 3, 8, LANES), f32),
             V((NZ, 3, 8, LANES), f32),
-            pltpu.SemaphoreType.DMA((96,)),
-            pltpu.SemaphoreType.DMA((96,)),
+            pltpu.SemaphoreType.DMA((112,)),
+            pltpu.SemaphoreType.DMA((112,)),
+            pltpu.SemaphoreType.DMA((g // 2,)),
+            pltpu.SemaphoreType.DMA((g // 2,)),
+            pltpu.SemaphoreType.DMA((NG,)),
+            pltpu.SemaphoreType.DMA((NG,)),
             pltpu.SemaphoreType.DMA((4,)),
         ],
         compiler_params=pltpu.CompilerParams(

time: 80.7 us -> 74.5 us (0.923)
  Pallas kernels: 77.9 us -> 72.4 us
    pallas_call x1, Pallas kernels: 75 us -> 69.6 us  [shards(): pl.pallas_call(kernel, out_shape=(V((3, g, rows + 8, LANES), f32), V((SLO...]
where the time goes in v7:
time: 74.5 us; the launch traced here: 74.4 us
  Pallas kernels  72.4 us (97%)
  between operations  1.93 us (3%)
    pallas_call x1, Pallas kernels, shards(): pl.pallas_call(kernel, out_shape=(V((3, g, rows + 8, LANES), f32), V((SLO...  69.6 us
    pallas_call x1, Pallas kernels, shards(): pl.pallas_call(finish, grid=(3,), out_shape=(jax.ShapeDtypeStruct((3, row...  2.86 us

profile of v7, /device:TPU:1, one launch (start us, length us, event | category | flops | bytes accessed | tf_op | source)
XLA Modules:
  0.0 74.4 jit_solution(14292624808231658809)
XLA Ops:
  1.9 69.6 %shard_map.85 = (f32[3,8,392,128]{3,2,1,0:T(8,128)S(1)}, f32[4,24,128]{2,1,0:T(8,128)S(1)}, f32[4,24,128]{2,1,0:T(8,128)S(1)}, f32[8,3,8,128]{3,2,1,0:T(8,128)S(1)}) custom-call(bf16[3,384,1024]{2,1,0:T(8,128)(2,1)} %streams_ref.1, f32[3,7,1024]{2,1,0:T(8,128)} %filters_ref.1, bf16[64,1024]{1,0:T(8,128)(2,1)} %bitcast.1, bf16[384,512]{1,0:T(8,128)(2,1)} %grad_ref.1, ...), custom_call_target="tpu_custom_call" | custom-call | flops 3221225472 | bytes 4718592 | tf_op jit(solution)/shard_map/pallas_call | solution.py:421
  71.5 2.9 %shard_map.86 = (bf16[3,384,1024]{2,1,0:T(8,128)(2,1)}, f32[3,4,1024]{2,1,0:T(4,128)}, f32[3,7,1024]{2,1,0:T(8,128)}) custom-call(s32[1]{0:T(128)S(6)} %copy.10.starts_ref, f32[3,8,392,128]{3,2,1,0:T(8,128)S(1)} %get-tuple-element.7.du_ref, f32[4,24,128]{2,1,0:T(8,128)S(1)} %get-tuple-element.8.inv_ref, f32[4,24,128]{2,1,0:T(8,128)S(1)} %get-tuple-element.9.scale_ref, ...), custom_call_target="tpu_custom_call" | custom-call | tf_op jit(solution)/shard_map/pallas_call | solution.py:467

commit v8 on v7

--- a/solution.py
+++ b/solution.py
@@ -14,6 +14,8 @@
 NG = NX * NC
 CH = 64
 SLOTS = 4
+WIDE = 512
+PER = WIDE // LANES
 STEP = 49
 VLIM = 54
 
@@ -197,16 +199,16 @@
         return 0
 
     def project(b, slot):
-        cols = pl.ds(pl.multiple_of(b * 256, 256), 256)
-        w = wt[:, :, :, :, cols].reshape(NZ * NG * 64, 256)
+        cols = pl.ds(pl.multiple_of(b * WIDE, WIDE), WIDE)
+        w = wt[:, :, :, :, cols].reshape(NZ * NG * 64, WIDE)
         dy = jnp.dot(gg[...], w, preferred_element_type=jnp.float32)
         dy = dy.astype(jnp.bfloat16).astype(jnp.float32)
-        dyb[slot, 0, :rows, :] = dy[:, :LANES]
-        dyb[slot, 1, :rows, :] = dy[:, LANES:]
+        for e in range(PER):
+            dyb[slot, e, :rows, :] = dy[:, e * LANES : (e + 1) * LANES]
 
     def gate(b, slot):
-        for e in range(2):
-            cg = 2 * b + e
+        for e in range(PER):
+            cg = PER * b + e
             for s in range(3):
                 acc = [jnp.zeros((8, LANES), jnp.float32)] * taps
                 window = [u32[s, cg, strided(8 - j), :] for j in range(1, taps)]
@@ -267,12 +269,12 @@
     arrived(flight["g04"])
     arrived(flight["g14"])
 
-    blocks = groups // 2
+    blocks = groups // PER
 
     def head_copy(b):
-        two = pl.ds(2 * b, 2)
+        some = pl.ds(PER * b, PER)
         return pltpu.make_async_remote_copy(
-            src_ref=head.at[:, two], dst_ref=heads_in.at[:, two], send_sem=hsend.at[b], recv_sem=hrecv.at[b],
+            src_ref=head.at[:, some], dst_ref=heads_in.at[:, some], send_sem=hsend.at[b], recv_sem=hrecv.at[b],
             device_id=(down, y), device_id_type=MESH,
         )
 
@@ -284,10 +286,10 @@
 
     def leave(b):
         head_copy(b).start()
-        for e in range(2):
-            @pl.when(2 * b + e != q)
+        for e in range(PER):
+            @pl.when(PER * b + e != q)
             def _():
-                term_copy(2 * b + e, q).start()
+                term_copy(PER * b + e, q).start()
 
     def both(b, _):
         gate(b - 1, (b + 1) % 2)
@@ -304,7 +306,7 @@
 
     def backward(b, _):
         head_copy(b).wait_recv()
-        lax.fori_loop(2 * b, 2 * b + 2, group_back, 0)
+        lax.fori_loop(PER * b, PER * b + PER, group_back, 0)
         return 0
 
     def group_back(cg, _):
@@ -435,7 +437,7 @@
             V((3, g, STEP, 8, LANES), f32),
             V((NZ, NX, NC, 64, channels), bf16),
             V((rows, NY * width), bf16),
-            V((2, 2, rows + 8, LANES), f32),
+            V((2, PER, rows + 8, LANES), f32),
             V((3, g, rows + 16, LANES), f32),
             V((3, g, 8, LANES), f32),
             V((3, g, 8, LANES), f32),

time: 74.5 us -> 74.4 us (level)
  no operation moved by 1% of the time
where the time goes in v8:
time: 74.4 us; the launch traced here: 74.3 us
  Pallas kernels  72.4 us (97%)
  between operations  1.93 us (3%)
    pallas_call x1, Pallas kernels, shards(): pl.pallas_call(kernel, out_shape=(V((3, g, rows + 8, LANES), f32), V((SLO...  69.5 us
    pallas_call x1, Pallas kernels, shards(): pl.pallas_call(finish, grid=(3,), out_shape=(jax.ShapeDtypeStruct((3, row...  2.86 us

profile of v8, /device:TPU:1, one launch (start us, length us, event | category | flops | bytes accessed | tf_op | source)
XLA Modules:
  0.0 74.3 jit_solution(7865747342898493772)
XLA Ops:
  1.9 69.5 %shard_map.85 = (f32[3,8,392,128]{3,2,1,0:T(8,128)S(1)}, f32[4,24,128]{2,1,0:T(8,128)S(1)}, f32[4,24,128]{2,1,0:T(8,128)S(1)}, f32[8,3,8,128]{3,2,1,0:T(8,128)S(1)}) custom-call(bf16[3,384,1024]{2,1,0:T(8,128)(2,1)} %streams_ref.1, f32[3,7,1024]{2,1,0:T(8,128)} %filters_ref.1, bf16[64,1024]{1,0:T(8,128)(2,1)} %bitcast.1, bf16[384,512]{1,0:T(8,128)(2,1)} %grad_ref.1, ...), custom_call_target="tpu_custom_call" | custom-call | flops 3221225472 | bytes 4718592 | tf_op jit(solution)/shard_map/pallas_call | solution.py:423
  71.4 2.9 %shard_map.86 = (bf16[3,384,1024]{2,1,0:T(8,128)(2,1)}, f32[3,4,1024]{2,1,0:T(4,128)}, f32[3,7,1024]{2,1,0:T(8,128)}) custom-call(s32[1]{0:T(128)S(6)} %copy.10.starts_ref, f32[3,8,392,128]{3,2,1,0:T(8,128)S(1)} %get-tuple-element.7.du_ref, f32[4,24,128]{2,1,0:T(8,128)S(1)} %get-tuple-element.8.inv_ref, f32[4,24,128]{2,1,0:T(8,128)S(1)} %get-tuple-element.9.scale_ref, ...), custom_call_target="tpu_custom_call" | custom-call | tf_op jit(solution)/shard_map/pallas_call | solution.py:469
